TPU v7x, 256 devices: a whole 4x4x8 slice. The times are simulated.
256 devices in a mesh: section: 8 (over y, x_lo), replica: 32 (over z, x_hi, core).
Axes of the slice: x: 4 (x_hi: 2, x_lo: 2; x = x_hi * 2 + x_lo), y: 4, z: 8, core: 2. Of those that a mesh axis runs over, the one named last changes fastest.
Arguments:
- master_old: float32 [16, 2048, 2048], P('section', 'replica'), may hold values from -0.125 to 0.125
- first_moment_old: float32 [16, 2048, 2048], P('section', 'replica'), may hold values from -180 to 180
- second_moment_old: float32 [16, 2048, 2048], P('section', 'replica'), may hold values from 100 to 10000
- layer_vectors: bfloat16 [16, 3, 2048], P('section'), may hold values from -1.5 to 1.5, as said below
- new_section: int32 [16], P('section'), may hold values from -1 to 7, as said below
- frozen: int32 [8], replicated, may hold values 0 or 1
- window_input: bfloat16 [8192, 2048], P('replica'), may hold values from -6 to 6
- cotangent: bfloat16 [8192, 2048], P('replica'), may hold values from -6 to 6
Outputs:
- master_new: float32 [8, 2048, 2048], P('section', 'replica')
- first_moment_new: float32 [8, 2048, 2048], P('section', 'replica')
- second_moment_new: float32 [8, 2048, 2048], P('section', 'replica')
Inputs may be any that keep to these rules, and one draw needn't show every extreme that they name: `new_section`: every section holds exactly one layer, in one of its 2 slots; the other slots hold -1. Every new section 0 to 7 is named once. A layer's new section differs from its old section by at most 1; in every draw the layer of section 0 moves to section 1 and the layer of section 7 moves to section 6. `layer_vectors`: row 0 of a slot is the projection's bias, row 1 the norm's gain (0.5 to 1.5), row 2 the norm's shift.
All inputs are finite; a program needn't handle non-finite values.
Results may differ from a plain program's by a relative error of at most 0.0044.
Values may be sent and summed in bfloat16 or wider, within the bound.
No kernel may reach another device: no remote copies, remote signals or barrier semaphores. Data moves between devices by JAX's collectives and lax.ppermute only.
A program may use at most 128 MiB of HBM per device.

v0:
```python
import jax
import jax.numpy as jnp
from jax import lax
from jax.sharding import PartitionSpec as P

MB = 4


FIRST_DECAY = 0.9
SECOND_DECAY = 0.999
STEP_SIZE = 0.01
EPSILON = 1e-08
FIRST_CORRECTION = 1.0 - 0.9**10
SECOND_CORRECTION = 1.0 - 0.999**10


def from_behind(value, axis, by):
    size = lax.axis_size(axis)
    pairs = [(i, i + by) for i in range(size) if 0 <= i + by < size]
    return lax.ppermute(value, axis, pairs)


def layer_norm(summed, norm_gain, norm_shift):
    center = summed - jnp.mean(summed, axis=-1, keepdims=True)
    spread = jnp.mean(center * center, axis=-1, keepdims=True)
    return center * lax.rsqrt(spread + 1e-05) * norm_gain + norm_shift


def smooth_gate(values):
    return jax.nn.gelu(values, approximate=True)


def layer_forward(layer_in, weight, vectors):
    linear = jnp.dot(layer_in, weight, preferred_element_type=jnp.float32) + vectors[0]
    summed = layer_in.astype(jnp.float32) + smooth_gate(linear)
    return (linear, layer_norm(summed, vectors[1], vectors[2]))


def layer_backward(layer_in, linear, upstream, weight, vectors):
    summed = layer_in.astype(jnp.float32) + smooth_gate(linear)
    _, pull_norm = jax.vjp(lambda values: layer_norm(values, vectors[1], vectors[2]), summed)
    (grad_summed,) = pull_norm(upstream.astype(jnp.float32))
    _, pull_gate = jax.vjp(smooth_gate, linear)
    (grad_linear,) = pull_gate(grad_summed)
    grad_linear = grad_linear.astype(jnp.bfloat16)
    input_grads = grad_summed + lax.dot_general(
        grad_linear, weight, (((1,), (1,)), ((), ())), preferred_element_type=jnp.float32
    )
    return (input_grads.astype(jnp.bfloat16), grad_linear)


def select_slot(stacked, mask):
    shaped = mask.reshape((-1,) + (1,) * (stacked.ndim - 1))
    return jnp.sum(jnp.where(shaped, stacked, jnp.zeros_like(stacked)), axis=0)


def join_parts(staying, rising, falling):
    return jax.tree.map(
        lambda staying_part, lower_part, upper_part: staying_part + lower_part + upper_part,
        staying,
        rising,
        falling,
    )


def move_layer(stay_mask, upper_mask, lower_mask, master_old, first_old, second_old, vector_old):
    rising = from_behind(
        (
            select_slot(master_old, upper_mask),
            select_slot(first_old, upper_mask),
            select_slot(second_old, upper_mask),
            select_slot(vector_old, upper_mask),
        ),
        "section",
        1,
    )
    falling = from_behind(
        (
            select_slot(master_old, lower_mask),
            select_slot(first_old, lower_mask),
            select_slot(second_old, lower_mask),
            select_slot(vector_old, lower_mask),
        ),
        "section",
        -1,
    )
    staying = (
        select_slot(master_old, stay_mask),
        select_slot(first_old, stay_mask),
        select_slot(second_old, stay_mask),
        select_slot(vector_old, stay_mask),
    )
    return join_parts(staying, tuple(rising), tuple(falling))


def store(stash, values, index, flag):
    previous = lax.dynamic_index_in_dim(stash, index, 0, keepdims=False)
    return lax.dynamic_update_index_in_dim(stash, jnp.where(flag, values, previous), index, 0)


def shards(
    master_old,
    first_moment_old,
    second_moment_old,
    layer_vectors,
    new_section,
    frozen,
    window_input,
    cotangent,
):
    section_index = lax.axis_index("section")
    sections = lax.axis_size("section")
    stay_mask = new_section == section_index
    upper_mask = new_section == section_index + 1
    lower_mask = new_section == section_index - 1
    master, first_state, second_state, vectors = move_layer(
        stay_mask,
        upper_mask,
        lower_mask,
        master_old,
        first_moment_old,
        second_moment_old,
        layer_vectors.astype(jnp.float32),
    )
    compute_rows = master.astype(jnp.bfloat16)
    full_weight = lax.all_gather(compute_rows, "replica", axis=0, tiled=True)
    features = full_weight.shape[1]
    row_count = window_input.shape[0] // MB
    batches = window_input.reshape(MB, row_count, features)
    upstream_batches = cotangent.reshape(MB, row_count, features)
    tick_total = MB + sections - 1

    def forward_tick(values):
        return layer_forward(values, full_weight, vectors)

    def forward_skip(values):
        zero_rows = jnp.zeros(values.shape, jnp.float32)
        return (zero_rows, zero_rows)

    received = jnp.zeros((row_count, features), jnp.bfloat16)
    stash_inputs = jnp.zeros((MB, row_count, features), jnp.bfloat16)
    stash_linear = jnp.zeros((MB, row_count, features), jnp.float32)
    for tick_number in range(tick_total):
        batch_index = tick_number - section_index
        in_range = (batch_index >= 0) & (batch_index < MB)
        batch_slot = jnp.clip(batch_index, 0, MB - 1)
        fresh_rows = lax.dynamic_index_in_dim(batches, batch_slot, 0, keepdims=False)
        layer_in = jnp.where(section_index == 0, fresh_rows, received)
        linear, output = lax.cond(in_range, forward_tick, forward_skip, layer_in)
        stash_inputs = store(stash_inputs, layer_in, batch_slot, in_range)
        stash_linear = store(stash_linear, linear, batch_slot, in_range)
        received = from_behind(output.astype(jnp.bfloat16), "section", 1)

    def backward_add(operands):
        input_grads, grad_linear = layer_backward(
            operands[0], operands[1], operands[2], full_weight, vectors
        )
        contribution = lax.dot_general(
            operands[0], grad_linear, (((0,), (0,)), ((), ())), preferred_element_type=jnp.float32
        )
        return (input_grads, grad_linear, operands[3] + contribution)

    def backward_keep(operands):
        zero_rows = jnp.zeros(operands[0].shape, jnp.bfloat16)
        return (zero_rows, zero_rows, operands[3])

    grad_total = jnp.zeros((features, features), jnp.float32)
    received = jnp.zeros((row_count, features), jnp.bfloat16)
    for tick_number in range(tick_total):
        batch_index = tick_number - (sections - 1 - section_index)
        in_range = (batch_index >= 0) & (batch_index < MB)
        batch_slot = jnp.clip(batch_index, 0, MB - 1)
        last_rows = lax.dynamic_index_in_dim(upstream_batches, batch_slot, 0, keepdims=False)
        upstream = jnp.where(section_index == sections - 1, last_rows, received)
        layer_in = lax.dynamic_index_in_dim(stash_inputs, batch_slot, 0, keepdims=False)
        linear = lax.dynamic_index_in_dim(stash_linear, batch_slot, 0, keepdims=False)
        input_grads, grad_linear, grad_total = lax.cond(
            in_range, backward_add, backward_keep, (layer_in, linear, upstream, grad_total)
        )
        received = from_behind(input_grads, "section", -1)
    grad_rows = lax.psum_scatter(
        grad_total.astype(jnp.bfloat16), "replica", scatter_dimension=0, tiled=True
    ).astype(jnp.float32)
    frozen_flag = lax.dynamic_index_in_dim(frozen, section_index, 0, keepdims=False)
    learning = frozen_flag == 0
    first_next = FIRST_DECAY * first_state + (1.0 - FIRST_DECAY) * grad_rows
    second_next = SECOND_DECAY * second_state + (1.0 - SECOND_DECAY) * grad_rows * grad_rows
    stepped = master - STEP_SIZE * (first_next / FIRST_CORRECTION) / (
        jnp.sqrt(second_next / SECOND_CORRECTION) + EPSILON
    )
    master_new = jnp.where(learning, stepped, master)
    first_moment_new = jnp.where(learning, first_next, first_state)
    second_moment_new = jnp.where(learning, second_next, second_state)
    return (master_new[None], first_moment_new[None], second_moment_new[None])


def solution(mesh):
    in_specs = (
        P("section", "replica", None),
        P("section", "replica", None),
        P("section", "replica", None),
        P("section", None, None),
        P("section"),
        P(),
        P("replica", None),
        P("replica", None),
    )
    out_specs = (
        P("section", "replica", None),
        P("section", "replica", None),
        P("section", "replica", None),
    )
    return jax.shard_map(shards, mesh=mesh, in_specs=in_specs, out_specs=out_specs, check_vma=False)
```

profile of v0, /device:TPU:6, one launch (start us, length us, event | category | flops | bytes accessed | tf_op | source)
XLA Modules:
  0.0 813.8 jit_solution(10966910562989717560)
XLA Ops:
  18.6 10.2 %collective-permute-done = f32[64,2048]{1,0:T(8,128)S(1)} collective-permute-done((f32[64,2048]{1,0:T(8,128)S(1)}, f32[64,2048]{1,0:T(8,128)S(1)}, u32[]{:S(2)}, u32[]{:S(2)}) %collective-permute-start) | collective-permute-done | bytes 524320 | tf_op jit(solution)/shard_map/ppermute | solution.py:20
  28.7 11.7 %collective-permute-done.1 = f32[64,2048]{1,0:T(8,128)S(1)} collective-permute-done((f32[64,2048]{1,0:T(8,128)S(1)}, f32[64,2048]{1,0:T(8,128)S(1)}, u32[]{:S(2)}, u32[]{:S(2)}) %collective-permute-start.1) | collective-permute-done | bytes 524320 | tf_op jit(solution)/shard_map/ppermute | solution.py:20
  52.2 91.8 %all-gather.2.cloned.1.call-done = bf16[2048,2048]{1,0:T(8,128)(2,1)} async-done(((bf16[64,2048]{1,0:T(8,128)(2,1)}), bf16[2048,2048]{1,0:T(8,128)(2,1)}) %all-gather.2.cloned.1.call-update) | async-done | bytes 8388624 | tf_op jit(solution)/shard_map/all_gather | solution.py:126
  148.2 9.6 %collective-permute-done.6 = bf16[64,2048]{1,0:T(8,128)(2,1)S(1)} collective-permute-done((bf16[64,2048]{1,0:T(8,128)(2,1)S(1)}, bf16[64,2048]{1,0:T(8,128)(2,1)S(1)}, u32[]{:S(2)}, u32[]{:S(2)}) %collective-permute-start.6) | collective-permute-done | bytes 262176 | tf_op jit(solution)/shard_map/ppermute | solution.py:20
  197.6 9.0 %conditional.25 = (f32[64,2048]{1,0:T(8,128)}, f32[64,2048]{1,0:T(8,128)S(1)}) conditional(s32[]{:T(128)} %convert_element_type.372, () %tuple.231, (bf16[64,2048]{1,0:T(8,128)(2,1)S(1)}, bf16[2048,2048]{1,0:T(8,128)(2,1)}, f32[3,2048]{1,0:T(4,128)S(1)}) %tuple.232), branch_computations={%region_21.22_spmd, %region_22.25_spmd} | conditional | flops 541982784 | bytes 11348240 | solution.py:149
  236.1 13.2 %collective-permute-start.11 = (bf16[64,2048]{1,0:T(8,128)(2,1)S(1)}, bf16[64,2048]{1,0:T(8,128)(2,1)S(1)}, u32[]{:S(2)}, u32[]{:S(2)}) collective-permute-start(bf16[64,2048]{1,0:T(8,128)(2,1)S(1)} %convert_element_type.377), channel_id=1, source_target_pairs={{0,32},{32,64},{64,96},{96,128},{128,160},{160,192},{192,224},{1,3... | collective-permute-start | bytes 786440 | tf_op jit(solution)/shard_map/ppermute | solution.py:20
  266.4 8.9 %collective-permute-start.13 = (bf16[64,2048]{1,0:T(8,128)(2,1)S(1)}, bf16[64,2048]{1,0:T(8,128)(2,1)S(1)}, u32[]{:S(2)}, u32[]{:S(2)}) collective-permute-start(bf16[64,2048]{1,0:T(8,128)(2,1)S(1)} %convert_element_type.381), channel_id=1, source_target_pairs={{0,32},{32,64},{64,96},{96,128},{128,160},{160,192},{192,224},{1,3... | collective-permute-start | bytes 786440 | tf_op jit(solution)/shard_map/ppermute | solution.py:20
  292.8 10.7 %collective-permute-start.15 = (bf16[64,2048]{1,0:T(8,128)(2,1)S(1)}, bf16[64,2048]{1,0:T(8,128)(2,1)S(1)}, u32[]{:S(2)}, u32[]{:S(2)}) collective-permute-start(bf16[64,2048]{1,0:T(8,128)(2,1)S(1)} %convert_element_type.385), channel_id=1, source_target_pairs={{0,32},{32,64},{64,96},{96,128},{128,160},{160,192},{192,224},{1,3... | collective-permute-start | bytes 786440 | tf_op jit(solution)/shard_map/ppermute | solution.py:20
  333.1 16.5 %collective-permute-done.17 = bf16[64,2048]{1,0:T(8,128)(2,1)S(1)} collective-permute-done((bf16[64,2048]{1,0:T(8,128)(2,1)}, bf16[64,2048]{1,0:T(8,128)(2,1)S(1)}, u32[]{:S(2)}, u32[]{:S(2)}) %collective-permute-start.17) | collective-permute-done | bytes 262176 | tf_op jit(solution)/shard_map/ppermute | solution.py:20
  352.4 8.9 %collective-permute-done.18 = bf16[64,2048]{1,0:T(8,128)(2,1)S(1)} collective-permute-done((bf16[64,2048]{1,0:T(8,128)(2,1)}, bf16[64,2048]{1,0:T(8,128)(2,1)S(1)}, u32[]{:S(2)}, u32[]{:S(2)}) %collective-permute-start.18) | collective-permute-done | bytes 262176 | tf_op jit(solution)/shard_map/ppermute | solution.py:20
  364.0 14.2 %collective-permute-done.19 = bf16[64,2048]{1,0:T(8,128)(2,1)S(1)} collective-permute-done((bf16[64,2048]{1,0:T(8,128)(2,1)}, bf16[64,2048]{1,0:T(8,128)(2,1)S(1)}, u32[]{:S(2)}, u32[]{:S(2)}) %collective-permute-start.19) | collective-permute-done | bytes 262176 | tf_op jit(solution)/shard_map/ppermute | solution.py:20
  391.3 111.1 %collective-permute-done.21 = bf16[64,2048]{1,0:T(8,128)(2,1)S(1)} collective-permute-done((bf16[64,2048]{1,0:T(8,128)(2,1)}, bf16[64,2048]{1,0:T(8,128)(2,1)S(1)}, u32[]{:S(2)}, u32[]{:S(2)}) %collective-permute-start.21) | collective-permute-done | bytes 262176 | tf_op jit(solution)/shard_map/ppermute | solution.py:20
  502.4 21.7 %conditional.39 = (bf16[64,2048]{1,0:T(8,128)(2,1)}, f32[2048,2048]{1,0:T(8,128)}) conditional(s32[]{:T(128)} %convert_element_type.357, f32[2048,2048]{1,0:T(8,128)} %get-tuple-element.1118, (s32[]{:T(128)}, bf16[4,64,2048]{2,1,0:T(8,128)(2,1)}, pred[64,2048]{1,0:T(8,128)(4,1)S(1)}, bf16[64,2048]{1,0:T(8,128)(2,1)S(1)}, f32[3,2048]{1,0:T(4,128)}, ...), branch_computations={%region_87.88_spmd, %region_88.93_spmd} | conditional | flops 1087504640 | bytes 74488424 | solution.py:177
  506.4 14.2 %convolution_add_fusion.22 = f32[2048,2048]{1,0:T(8,128)} fusion(f32[2048,2048]{1,0:T(8,128)} %get-tuple-element.1009, bf16[4,64,2048]{2,1,0:T(8,128)(2,1)S(1)} %get-tuple-element.1006, s32[]{:T(128)S(6)} %min.62, f32[64,2048]{1,0:T(8,128)S(1)} %get-tuple-element.1195, f32[4,64,2048]{2,1,0:T(8,128)S(1)} %get-tuple-element.1007, ...), kind=kOutput, calls=%fused_computation.331 | convolution fusion | flops 543817728 | bytes 34866688 | tf_op jit(solution)/shard_map/cond/branch_1_fun/dot_general | solution.py:158
  533.4 21.5 %conditional.40 = (bf16[64,2048]{1,0:T(8,128)(2,1)}, f32[2048,2048]{1,0:T(8,128)}) conditional(s32[]{:T(128)} %convert_element_type.356, f32[2048,2048]{1,0:T(8,128)} %get-tuple-element.1120, (s32[]{:T(128)}, bf16[4,64,2048]{2,1,0:T(8,128)(2,1)}, pred[64,2048]{1,0:T(8,128)(4,1)S(1)}, bf16[64,2048]{1,0:T(8,128)(2,1)S(1)}, f32[3,2048]{1,0:T(4,128)}, ...), branch_computations={%region_93.94_spmd, %region_94.99_spmd} | conditional | flops 1087504640 | bytes 74488424 | solution.py:177
  537.3 14.2 %convolution_add_fusion.24 = f32[2048,2048]{1,0:T(8,128)} fusion(f32[2048,2048]{1,0:T(8,128)} %get-tuple-element.1018, bf16[4,64,2048]{2,1,0:T(8,128)(2,1)S(1)} %get-tuple-element.1015, s32[]{:T(128)S(6)} %min.63, f32[64,2048]{1,0:T(8,128)S(1)} %get-tuple-element.1199, f32[4,64,2048]{2,1,0:T(8,128)S(1)} %get-tuple-element.1016, ...), kind=kOutput, calls=%fused_computation.361 | convolution fusion | flops 543817728 | bytes 34866688 | tf_op jit(solution)/shard_map/cond/branch_1_fun/dot_general | solution.py:158
  564.3 21.7 %conditional.41 = (bf16[64,2048]{1,0:T(8,128)(2,1)}, f32[2048,2048]{1,0:T(8,128)}) conditional(s32[]{:T(128)} %convert_element_type.355, f32[2048,2048]{1,0:T(8,128)} %get-tuple-element.1122, (s32[]{:T(128)}, bf16[4,64,2048]{2,1,0:T(8,128)(2,1)}, pred[64,2048]{1,0:T(8,128)(4,1)S(1)}, bf16[64,2048]{1,0:T(8,128)(2,1)S(1)}, f32[3,2048]{1,0:T(4,128)}, ...), branch_computations={%region_99.100_spmd, %region_100.105_spmd} | conditional | flops 1087504640 | bytes 74488424 | solution.py:177
  568.4 14.2 %convolution_add_fusion.26 = f32[2048,2048]{1,0:T(8,128)} fusion(f32[2048,2048]{1,0:T(8,128)} %get-tuple-element.1027, bf16[4,64,2048]{2,1,0:T(8,128)(2,1)S(1)} %get-tuple-element.1024, s32[]{:T(128)S(6)} %min.64, f32[64,2048]{1,0:T(8,128)S(1)} %get-tuple-element.1203, f32[4,64,2048]{2,1,0:T(8,128)S(1)} %get-tuple-element.1025, ...), kind=kOutput, calls=%fused_computation.391 | convolution fusion | flops 543817728 | bytes 34866688 | tf_op jit(solution)/shard_map/cond/branch_1_fun/dot_general | solution.py:158
  595.3 21.5 %conditional.42 = (bf16[64,2048]{1,0:T(8,128)(2,1)}, f32[2048,2048]{1,0:T(8,128)}) conditional(s32[]{:T(128)} %convert_element_type.354, f32[2048,2048]{1,0:T(8,128)} %get-tuple-element.1124, (s32[]{:T(128)}, bf16[4,64,2048]{2,1,0:T(8,128)(2,1)}, pred[64,2048]{1,0:T(8,128)(4,1)S(1)}, bf16[64,2048]{1,0:T(8,128)(2,1)S(1)}, f32[3,2048]{1,0:T(4,128)}, ...), branch_computations={%region_105.106_spmd, %region_106.111_spmd} | conditional | flops 1087504640 | bytes 74488424 | solution.py:177
  599.2 14.2 %convolution_add_fusion.28 = f32[2048,2048]{1,0:T(8,128)} fusion(f32[2048,2048]{1,0:T(8,128)} %get-tuple-element.1036, bf16[4,64,2048]{2,1,0:T(8,128)(2,1)S(1)} %get-tuple-element.1033, s32[]{:T(128)S(6)} %min.65, f32[64,2048]{1,0:T(8,128)S(1)} %get-tuple-element.1207, f32[4,64,2048]{2,1,0:T(8,128)S(1)} %get-tuple-element.1034, ...), kind=kOutput, calls=%fused_computation.421 | convolution fusion | flops 543817728 | bytes 34866688 | tf_op jit(solution)/shard_map/cond/branch_1_fun/dot_general | solution.py:158
  618.8 10.3 %collective-permute-done.25 = bf16[64,2048]{1,0:T(8,128)(2,1)S(1)} collective-permute-done((bf16[64,2048]{1,0:T(8,128)(2,1)}, bf16[64,2048]{1,0:T(8,128)(2,1)S(1)}, u32[]{:S(2)}, u32[]{:S(2)}) %collective-permute-start.25) | collective-permute-done | bytes 262176 | tf_op jit(solution)/shard_map/ppermute | solution.py:20
  629.3 9.1 %convert_element_type.387 = bf16[2048,2048]{1,0:T(8,128)(2,1)} convert(f32[2048,2048]{1,0:T(8,128)} %get-tuple-element.1394) | non-fusion elementwise | flops 4194304 | bytes 25165824 | tf_op jit(solution)/shard_map/convert_element_type | solution.py:182
  642.6 18.8 %collective-permute-start.27 = (f32[64,2048]{1,0:T(8,128)}, f32[64,2048]{1,0:T(8,128)}, u32[]{:S(2)}, u32[]{:S(2)}) collective-permute-start(f32[64,2048]{1,0:T(8,128)} %get-tuple-element.1162), channel_id=1, source_target_pairs={{32,0},{64,32},{96,64},{128,96},{160,128},{192,160},{224,192},{33,... | collective-permute-start | bytes 1572872 | tf_op jit(solution)/shard_map/ppermute | solution.py:20
  675.1 127.9 %reduce-scatter.2.cloned.1.call-done = bf16[64,2048]{1,0:T(8,128)(2,1)} async-done(((bf16[2048,2048]{1,0:T(8,128)(2,1)}), bf16[64,2048]{1,0:T(8,128)(2,1)}) %reduce-scatter.2.cloned.1.call-update) | async-done | bytes 262160 | tf_op jit(solution)/shard_map/reduce_scatter | solution.py:181
  (250 shorter events, 311.1 us)
Async XLA Ops:
  7.2 136.9 %all-gather.2.cloned.1.call-start = ((), (), s32[]{:S(2)}) async-start(), calls=%async_computation.1 | async-start | bytes 8650752 | tf_op jit(solution)/shard_map/all_gather | solution.py:126
  12.7 16.1 %collective-permute-start = (f32[64,2048]{1,0:T(8,128)S(1)}, f32[64,2048]{1,0:T(8,128)S(1)}, u32[]{:S(2)}, u32[]{:S(2)}) collective-permute-start(f32[64,2048]{1,0:T(8,128)S(1)} %get-tuple-element.1156), channel_id=1, source_target_pairs={{0,32},{32,64},{64,96},{96,128},{128,160},{160,192},{192,224},{1,3... | collective-permute-start | bytes 1572872 | tf_op jit(solution)/shard_map/ppermute | solution.py:20
  16.4 24.0 %collective-permute-start.1 = (f32[64,2048]{1,0:T(8,128)S(1)}, f32[64,2048]{1,0:T(8,128)S(1)}, u32[]{:S(2)}, u32[]{:S(2)}) collective-permute-start(f32[64,2048]{1,0:T(8,128)S(1)} %get-tuple-element.1158), channel_id=1, source_target_pairs={{32,0},{64,32},{96,64},{128,96},{160,128},{192,160},{224,192},{33,... | collective-permute-start | bytes 1572872 | tf_op jit(solution)/shard_map/ppermute | solution.py:20
  41.4 761.7 %reduce-scatter.2.cloned.1.call-start = ((), (), s32[]{:S(2)}) async-start(), calls=%async_computation.2 | async-start | bytes 8650752 | tf_op jit(solution)/shard_map/reduce_scatter | solution.py:181
  144.3 13.5 %collective-permute-start.6 = (bf16[64,2048]{1,0:T(8,128)(2,1)S(1)}, bf16[64,2048]{1,0:T(8,128)(2,1)S(1)}, u32[]{:S(2)}, u32[]{:S(2)}) collective-permute-start(bf16[64,2048]{1,0:T(8,128)(2,1)S(1)} %convert_element_type.367), channel_id=1, source_target_pairs={{0,32},{32,64},{64,96},{96,128},{128,160},{160,192},{192,224},{1,3... | collective-permute-start | bytes 786440 | tf_op jit(solution)/shard_map/ppermute | solution.py:20
  167.8 9.9 %collective-permute-start.7 = (bf16[64,2048]{1,0:T(8,128)(2,1)S(1)}, bf16[64,2048]{1,0:T(8,128)(2,1)S(1)}, u32[]{:S(2)}, u32[]{:S(2)}) collective-permute-start(bf16[64,2048]{1,0:T(8,128)(2,1)S(1)} %convert_element_type.369), channel_id=1, source_target_pairs={{0,32},{32,64},{64,96},{96,128},{128,160},{160,192},{192,224},{1,3... | collective-permute-start | bytes 786440 | tf_op jit(solution)/shard_map/ppermute | solution.py:20
  236.1 17.1 %collective-permute-start.11 = (bf16[64,2048]{1,0:T(8,128)(2,1)S(1)}, bf16[64,2048]{1,0:T(8,128)(2,1)S(1)}, u32[]{:S(2)}, u32[]{:S(2)}) collective-permute-start(bf16[64,2048]{1,0:T(8,128)(2,1)S(1)} %convert_element_type.377), channel_id=1, source_target_pairs={{0,32},{32,64},{64,96},{96,128},{128,160},{160,192},{192,224},{1,3... | collective-permute-start | bytes 786440 | tf_op jit(solution)/shard_map/ppermute | solution.py:20
  266.4 12.8 %collective-permute-start.13 = (bf16[64,2048]{1,0:T(8,128)(2,1)S(1)}, bf16[64,2048]{1,0:T(8,128)(2,1)S(1)}, u32[]{:S(2)}, u32[]{:S(2)}) collective-permute-start(bf16[64,2048]{1,0:T(8,128)(2,1)S(1)} %convert_element_type.381), channel_id=1, source_target_pairs={{0,32},{32,64},{64,96},{96,128},{128,160},{160,192},{192,224},{1,3... | collective-permute-start | bytes 786440 | tf_op jit(solution)/shard_map/ppermute | solution.py:20
  281.6 9.2 %collective-permute-start.14 = (bf16[64,2048]{1,0:T(8,128)(2,1)S(1)}, bf16[64,2048]{1,0:T(8,128)(2,1)S(1)}, u32[]{:S(2)}, u32[]{:S(2)}) collective-permute-start(bf16[64,2048]{1,0:T(8,128)(2,1)S(1)} %convert_element_type.383), channel_id=1, source_target_pairs={{0,32},{32,64},{64,96},{96,128},{128,160},{160,192},{192,224},{1,3... | collective-permute-start | bytes 786440 | tf_op jit(solution)/shard_map/ppermute | solution.py:20
  292.8 14.5 %collective-permute-start.15 = (bf16[64,2048]{1,0:T(8,128)(2,1)S(1)}, bf16[64,2048]{1,0:T(8,128)(2,1)S(1)}, u32[]{:S(2)}, u32[]{:S(2)}) collective-permute-start(bf16[64,2048]{1,0:T(8,128)(2,1)S(1)} %convert_element_type.385), channel_id=1, source_target_pairs={{0,32},{32,64},{64,96},{96,128},{128,160},{160,192},{192,224},{1,3... | collective-permute-start | bytes 786440 | tf_op jit(solution)/shard_map/ppermute | solution.py:20
  319.8 9.8 %collective-permute-start.16 = (bf16[64,2048]{1,0:T(8,128)(2,1)}, bf16[64,2048]{1,0:T(8,128)(2,1)S(1)}, u32[]{:S(2)}, u32[]{:S(2)}) collective-permute-start(bf16[64,2048]{1,0:T(8,128)(2,1)} %get-tuple-element.1109), channel_id=1, source_target_pairs={{32,0},{64,32},{96,64},{128,96},{160,128},{192,160},{224,192},{33,... | collective-permute-start | bytes 786440 | tf_op jit(solution)/shard_map/ppermute | solution.py:20
  330.4 19.2 %collective-permute-start.17 = (bf16[64,2048]{1,0:T(8,128)(2,1)}, bf16[64,2048]{1,0:T(8,128)(2,1)S(1)}, u32[]{:S(2)}, u32[]{:S(2)}) collective-permute-start(bf16[64,2048]{1,0:T(8,128)(2,1)} %get-tuple-element.1111), channel_id=1, source_target_pairs={{32,0},{64,32},{96,64},{128,96},{160,128},{192,160},{224,192},{33,... | collective-permute-start | bytes 786440 | tf_op jit(solution)/shard_map/ppermute | solution.py:20
  350.5 10.8 %collective-permute-start.18 = (bf16[64,2048]{1,0:T(8,128)(2,1)}, bf16[64,2048]{1,0:T(8,128)(2,1)S(1)}, u32[]{:S(2)}, u32[]{:S(2)}) collective-permute-start(bf16[64,2048]{1,0:T(8,128)(2,1)} %get-tuple-element.1113), channel_id=1, source_target_pairs={{32,0},{64,32},{96,64},{128,96},{160,128},{192,160},{224,192},{33,... | collective-permute-start | bytes 786440 | tf_op jit(solution)/shard_map/ppermute | solution.py:20
  362.0 16.1 %collective-permute-start.19 = (bf16[64,2048]{1,0:T(8,128)(2,1)}, bf16[64,2048]{1,0:T(8,128)(2,1)S(1)}, u32[]{:S(2)}, u32[]{:S(2)}) collective-permute-start(bf16[64,2048]{1,0:T(8,128)(2,1)} %get-tuple-element.1115), channel_id=1, source_target_pairs={{32,0},{64,32},{96,64},{128,96},{160,128},{192,160},{224,192},{33,... | collective-permute-start | bytes 786440 | tf_op jit(solution)/shard_map/ppermute | solution.py:20
  379.3 9.4 %collective-permute-start.20 = (bf16[64,2048]{1,0:T(8,128)(2,1)}, bf16[64,2048]{1,0:T(8,128)(2,1)S(1)}, u32[]{:S(2)}, u32[]{:S(2)}) collective-permute-start(bf16[64,2048]{1,0:T(8,128)(2,1)} %get-tuple-element.1117), channel_id=1, source_target_pairs={{32,0},{64,32},{96,64},{128,96},{160,128},{192,160},{224,192},{33,... | collective-permute-start | bytes 786440 | tf_op jit(solution)/shard_map/ppermute | solution.py:20
  389.4 113.0 %collective-permute-start.21 = (bf16[64,2048]{1,0:T(8,128)(2,1)}, bf16[64,2048]{1,0:T(8,128)(2,1)S(1)}, u32[]{:S(2)}, u32[]{:S(2)}) collective-permute-start(bf16[64,2048]{1,0:T(8,128)(2,1)} %get-tuple-element.1119), channel_id=1, source_target_pairs={{32,0},{64,32},{96,64},{128,96},{160,128},{192,160},{224,192},{33,... | collective-permute-start | bytes 786440 | tf_op jit(solution)/shard_map/ppermute | solution.py:20
  524.1 9.4 %collective-permute-start.22 = (bf16[64,2048]{1,0:T(8,128)(2,1)}, bf16[64,2048]{1,0:T(8,128)(2,1)S(1)}, u32[]{:S(2)}, u32[]{:S(2)}) collective-permute-start(bf16[64,2048]{1,0:T(8,128)(2,1)} %get-tuple-element.1121), channel_id=1, source_target_pairs={{32,0},{64,32},{96,64},{128,96},{160,128},{192,160},{224,192},{33,... | collective-permute-start | bytes 786440 | tf_op jit(solution)/shard_map/ppermute | solution.py:20
  554.9 9.4 %collective-permute-start.23 = (bf16[64,2048]{1,0:T(8,128)(2,1)}, bf16[64,2048]{1,0:T(8,128)(2,1)S(1)}, u32[]{:S(2)}, u32[]{:S(2)}) collective-permute-start(bf16[64,2048]{1,0:T(8,128)(2,1)} %get-tuple-element.1123), channel_id=1, source_target_pairs={{32,0},{64,32},{96,64},{128,96},{160,128},{192,160},{224,192},{33,... | collective-permute-start | bytes 786440 | tf_op jit(solution)/shard_map/ppermute | solution.py:20
  586.0 9.4 %collective-permute-start.24 = (bf16[64,2048]{1,0:T(8,128)(2,1)}, bf16[64,2048]{1,0:T(8,128)(2,1)S(1)}, u32[]{:S(2)}, u32[]{:S(2)}) collective-permute-start(bf16[64,2048]{1,0:T(8,128)(2,1)} %get-tuple-element.1125), channel_id=1, source_target_pairs={{32,0},{64,32},{96,64},{128,96},{160,128},{192,160},{224,192},{33,... | collective-permute-start | bytes 786440 | tf_op jit(solution)/shard_map/ppermute | solution.py:20
  616.8 12.2 %collective-permute-start.25 = (bf16[64,2048]{1,0:T(8,128)(2,1)}, bf16[64,2048]{1,0:T(8,128)(2,1)S(1)}, u32[]{:S(2)}, u32[]{:S(2)}) collective-permute-start(bf16[64,2048]{1,0:T(8,128)(2,1)} %get-tuple-element.1127), channel_id=1, source_target_pairs={{32,0},{64,32},{96,64},{128,96},{160,128},{192,160},{224,192},{33,... | collective-permute-start | bytes 786440 | tf_op jit(solution)/shard_map/ppermute | solution.py:20
  638.5 26.1 %collective-permute-start.2 = (f32[64,2048]{1,0:T(8,128)}, f32[64,2048]{1,0:T(8,128)}, u32[]{:S(2)}, u32[]{:S(2)}) collective-permute-start(f32[64,2048]{1,0:T(8,128)} %get-tuple-element.1167), channel_id=1, source_target_pairs={{0,32},{32,64},{64,96},{96,128},{128,160},{160,192},{192,224},{1,3... | collective-permute-start | bytes 1572872 | tf_op jit(solution)/shard_map/ppermute | solution.py:20
  640.7 29.0 %collective-permute-start.26 = (f32[64,2048]{1,0:T(8,128)}, f32[64,2048]{1,0:T(8,128)}, u32[]{:S(2)}, u32[]{:S(2)}) collective-permute-start(f32[64,2048]{1,0:T(8,128)} %get-tuple-element.1164), channel_id=1, source_target_pairs={{0,32},{32,64},{64,96},{96,128},{128,160},{160,192},{192,224},{1,3... | collective-permute-start | bytes 1572872 | tf_op jit(solution)/shard_map/ppermute | solution.py:20
  642.6 27.0 %collective-permute-start.27 = (f32[64,2048]{1,0:T(8,128)}, f32[64,2048]{1,0:T(8,128)}, u32[]{:S(2)}, u32[]{:S(2)}) collective-permute-start(f32[64,2048]{1,0:T(8,128)} %get-tuple-element.1162), channel_id=1, source_target_pairs={{32,0},{64,32},{96,64},{128,96},{160,128},{192,160},{224,192},{33,... | collective-permute-start | bytes 1572872 | tf_op jit(solution)/shard_map/ppermute | solution.py:20
  661.4 13.7 %collective-permute-start.3 = (f32[64,2048]{1,0:T(8,128)S(1)}, f32[64,2048]{1,0:T(8,128)}, u32[]{:S(2)}, u32[]{:S(2)}) collective-permute-start(f32[64,2048]{1,0:T(8,128)S(1)} %copy-done.10), channel_id=1, source_target_pairs={{32,0},{64,32},{96,64},{128,96},{160,128},{192,160},{224,192},{33,... | collective-permute-start | bytes 1572872 | tf_op jit(solution)/shard_map/ppermute | solution.py:20
  (27 other events, 1492.3 us)
Sparse Core Ops, SparseCore 0:
  41.5 102.5 all-gather.1
  638.6 164.4 reduce-scatter.1
where the time goes:
time: 826 us; the launch traced here: 814 us
  waiting for transfers between devices  486 us (59%)
  starting transfers between devices  117 us (14%)
  matrix products  94.5 us (11%)
  other arithmetic  66.7 us (8%)
  local copies, waits for them, and re-layouts  31 us (4%)
  between operations  15.9 us (2%)
    ppermute x28, waiting for transfers between devices, from_behind(): return lax.ppermute(value, axis, pairs)  266 us
    reduce_scatter x1, waiting for transfers between devices, shards(): lax.psum_scatter(grad_total.astype(jnp.bfloat16), 'replica', scatter_dime...  128 us
    ppermute x28, starting transfers between devices, from_behind(): return lax.ppermute(value, axis, pairs)  117 us
    all_gather x1, waiting for transfers between devices, shards(): full_weight = lax.all_gather(compute_rows, 'replica', axis=0, tiled=True)  91.8 us
    dot_general x4, matrix products, backward_add(): lax.dot_general(operands[0], grad_linear, (((0,), (0,)), ((), ())), prefe...  56.8 us
    dot_general x4, matrix products, layer_forward(): jnp.dot(layer_in, weight, preferred_element_type=jnp.float32) + vectors[0]  24.1 us
    dynamic_update_slice x21, other arithmetic, store(): lax.dynamic_update_index_in_dim(stash, jnp.where(flag, values, previous),...  23.2 us
  transfers between devices with their start and end apart: 30, of which 27 were waited for; matrix products, arithmetic and copies ran while one was open for 3% of the time, Pallas kernels for 0%

commit v1 on v0

v1 whole, which is shorter than its diff:
```python
import functools
import jax
import jax.numpy as jnp
from jax import lax
from jax.experimental import pallas as pl
from jax.experimental.pallas import tpu as pltpu
from jax.sharding import PartitionSpec as P

BF16 = jnp.bfloat16
F32 = jnp.float32
D = 2048
NZ = 8
VMEM_LIMIT = 48 * 1024 * 1024
GELU_K = 0.7978845608028654


def weight_copies(near, far, w_scr, sems, z_me, x_me, core):
    groups = {}
    for side, msgs in ((0, near), (1, far)):
        owner = core if side == 0 else 1 - core
        for piece, dx, dz, half in msgs:
            x = lax.rem(x_me + dx + 4, 4)
            z = lax.rem(z_me + dz + 8, 8)
            row = pl.multiple_of(((z * 2 + x // 2) * 2 + owner) * 64 + half * 32, 32)
            slot = dx % 2
            k = dz % 8
            groups.setdefault((slot, k), []).append(
                pltpu.make_async_copy(piece, w_scr.at[slot, pl.ds(row, 32), :], sems.at[slot, k])
            )
    return groups


def message_pieces(refs):
    pieces = []
    z_steps = (0, -1, 1, -2, 2, -3, 3)
    x_order = (0, -1, 1, 2)
    head, tail = refs[:9], refs[9:]
    for ref, dz in zip(head[:7], z_steps):
        for at, dx in enumerate(x_order):
            pieces.append((ref.at[at], dx, dz, 0))
    for at, dx in enumerate(x_order):
        ref = head[7] if at < 2 else head[8]
        pieces.append((ref.at[at % 2], dx, 4, 0))
    order = (0, -1, 1, -2, 2, -3, 3, 4)
    for ref, dx in zip(tail[:3], (0, -1, 1)):
        for at, dz in enumerate(order):
            pieces.append((ref.at[at], dx, dz, 1))
    for at, dz in enumerate(order):
        ref = tail[3] if at < 4 else tail[4]
        pieces.append((ref.at[at % 4], 2, dz, 1))
    return pieces


def gelu(u):
    return 0.5 * u * (1.0 + jnp.tanh(GELU_K * (u + 0.044715 * (u * u * u))))


def gelu_slope(u):
    t = jnp.tanh(GELU_K * (u + 0.044715 * (u * u * u)))
    return 0.5 * (1.0 + t) + 0.5 * u * (1.0 - t * t) * (GELU_K * (1.0 + 3 * 0.044715 * (u * u)))


def norm_parts(z):
    center = z - jnp.mean(z, axis=-1, keepdims=True)
    spread = jnp.mean(center * center, axis=-1, keepdims=True)
    return center, lax.rsqrt(spread + 1e-5)


def issue(groups, first):
    def start(slot):
        for k in range(NZ):
            for copy in groups[slot, k]:
                copy.start()

    @pl.when(first == 0)
    def _():
        start(0)
        start(1)

    @pl.when(first == 1)
    def _():
        start(1)
        start(0)


def wait_block(w_scr, sems, slot, k, z):
    rows = w_scr.at[slot, pl.ds(pl.multiple_of(z * 256, 256), 256), :]
    pltpu.make_async_copy(rows, rows, sems.at[slot, k]).wait()


def forward_kernel(n_msgs, rows, ctl, *refs):
    near, far = refs[:n_msgs], refs[n_msgs:2 * n_msgs]
    window, recv, vec, xs_in, ls_in, act, xs, ls, w_scr, x_scr, lin_scr, sems, sem_x, sem_o = refs[2 * n_msgs:]
    del xs_in, ls_in
    active, stage, batch, x_me, z_me, core, first, xl = (ctl[i] for i in range(8))

    @pl.when(active == 1)
    def _():
        groups = weight_copies(message_pieces(near), message_pieces(far), w_scr, sems, z_me, x_me, core)
        per_half = window.shape[0] // 2
        at = pl.multiple_of(batch * rows, rows)

        @pl.when(stage == 0)
        def _():
            src = window.at[pl.ds(pl.multiple_of(xl * per_half + batch * rows, rows), rows), :]
            pltpu.make_async_copy(src, x_scr.at[0], sem_x).start()

        @pl.when(stage != 0)
        def _():
            pltpu.make_async_copy(recv, x_scr.at[0], sem_x).start()

        issue(groups, first)
        pltpu.make_async_copy(recv, x_scr.at[0], sem_x).wait()
        outs = []
        for layer in range(2):
            slot = first ^ layer
            lin_scr[layer] = jnp.broadcast_to(vec[layer, 0:1, :], (rows, D))
            for k in range(NZ):
                z = lax.rem(z_me + k, NZ)
                wait_block(w_scr, sems, slot, k, z)
                cols = pl.ds(pl.multiple_of(z * 256, 256), 256)
                lin_scr[layer] += jnp.dot(
                    x_scr[layer, :, cols], w_scr[slot, cols, :], preferred_element_type=F32
                )
            lin = lin_scr[layer]
            center, scale = norm_parts(x_scr[layer].astype(F32) + gelu(lin))
            y = (center * scale * vec[layer, 1:2, :] + vec[layer, 2:3, :]).astype(BF16)
            if layer == 0:
                x_scr[1] = y
            else:
                act[...] = y
            for src, dst, n in ((x_scr, xs, 0), (lin_scr, ls, 1)):
                copy = pltpu.make_async_copy(src.at[layer], dst.at[layer, pl.ds(at, rows), :], sem_o.at[layer, n])
                copy.start()
                outs.append(copy)
        for copy in outs:
            copy.wait()


def backward_kernel(n_msgs, rows, ctl, *refs):
    near, far = refs[:n_msgs], refs[n_msgs:2 * n_msgs]
    cot, recv, vec, xs, ls, ds_in, back, ds, w_scr, g_scr, x_scr, lin_scr, dz_scr, dl_scr, sems, sem_x, sem_o = refs[2 * n_msgs:]
    del ds_in
    active, stage, batch, x_me, z_me, core, first, xl = (ctl[i] for i in range(8))

    @pl.when(active == 1)
    def _():
        groups = weight_copies(message_pieces(near), message_pieces(far), w_scr, sems, z_me, x_me, core)
        per_half = cot.shape[0] // 2
        at = pl.multiple_of(batch * rows, rows)

        @pl.when(stage == 3)
        def _():
            src = cot.at[pl.ds(pl.multiple_of(xl * per_half + batch * rows, rows), rows), :]
            pltpu.make_async_copy(src, g_scr, sem_x.at[2, 0]).start()

        @pl.when(stage != 3)
        def _():
            pltpu.make_async_copy(recv, g_scr, sem_x.at[2, 0]).start()

        loads = {}
        for layer in (1, 0):
            loads[layer] = (
                pltpu.make_async_copy(xs.at[layer, pl.ds(at, rows), :], x_scr.at[layer], sem_x.at[layer, 0]),
                pltpu.make_async_copy(ls.at[layer, pl.ds(at, rows), :], lin_scr.at[layer], sem_x.at[layer, 1]),
            )
            for copy in loads[layer]:
                copy.start()
        issue(groups, 1 - first)
        pltpu.make_async_copy(recv, g_scr, sem_x.at[2, 0]).wait()
        outs = []
        for layer in (1, 0):
            slot = first ^ layer
            for copy in loads[layer]:
                copy.wait()
            lin = lin_scr[layer]
            center, scale = norm_parts(x_scr[layer].astype(F32) + gelu(lin))
            unit = center * scale
            g = g_scr[...].astype(F32) * vec[layer, 1:2, :]
            dz = scale * (g - jnp.mean(g, axis=-1, keepdims=True) - unit * jnp.mean(g * unit, axis=-1, keepdims=True))
            dz_scr[...] = dz
            dl_scr[layer] = (dz * gelu_slope(lin)).astype(BF16)
            copy = pltpu.make_async_copy(dl_scr.at[layer], ds.at[layer, pl.ds(at, rows), :], sem_o.at[layer])
            copy.start()
            outs.append(copy)
            for k in range(NZ):
                z = lax.rem(z_me + k, NZ)
                wait_block(w_scr, sems, slot, k, z)
                cols = pl.ds(pl.multiple_of(z * 256, 256), 256)

                def step():
                    down = lax.dot_general(
                        dl_scr[layer], w_scr[slot, cols, :], (((1,), (1,)), ((), ())), preferred_element_type=F32
                    )
                    y = (dz_scr[:, cols] + down).astype(BF16)
                    if layer == 1:
                        g_scr[:, cols] = y
                    else:
                        back[:, cols] = y

                if layer == 1:
                    step()
                else:
                    pl.when(stage != 0)(step)
        for copy in outs:
            copy.wait()


def forward_call(ctl, near, far, window, recv, vec, xs, ls):
    rows = recv.shape[0]
    n = len(near)
    any_spec = pl.BlockSpec(memory_space=pl.ANY)
    vm = pl.BlockSpec(memory_space=pltpu.VMEM)
    return pl.pallas_call(
        functools.partial(forward_kernel, n, rows),
        out_shape=(
            jax.ShapeDtypeStruct((rows, D), BF16),
            jax.ShapeDtypeStruct(xs.shape, xs.dtype),
            jax.ShapeDtypeStruct(ls.shape, ls.dtype),
        ),
        in_specs=[pl.BlockSpec(memory_space=pltpu.SMEM)] + [any_spec] * (2 * n + 2) + [vm] + [any_spec] * 2,
        out_specs=(vm, any_spec, any_spec),
        scratch_shapes=[
            pltpu.VMEM((2, D, D), BF16),
            pltpu.VMEM((2, rows, D), BF16),
            pltpu.VMEM((2, rows, D), F32),
            pltpu.SemaphoreType.DMA((2, NZ)),
            pltpu.SemaphoreType.DMA,
            pltpu.SemaphoreType.DMA((2, 2)),
        ],
        input_output_aliases={2 * n + 4: 1, 2 * n + 5: 2},
        compiler_params=pltpu.CompilerParams(vmem_limit_bytes=VMEM_LIMIT),
        cost_estimate=pl.CostEstimate(flops=4 * rows * D * D, bytes_accessed=4 * D * D, transcendentals=2 * rows * D),
        name="forward_tick",
    )(ctl, *near, *far, window, recv, vec, xs, ls)


def backward_call(ctl, near, far, cot, recv, vec, xs, ls, ds):
    rows = recv.shape[0]
    n = len(near)
    any_spec = pl.BlockSpec(memory_space=pl.ANY)
    vm = pl.BlockSpec(memory_space=pltpu.VMEM)
    return pl.pallas_call(
        functools.partial(backward_kernel, n, rows),
        out_shape=(jax.ShapeDtypeStruct((rows, D), BF16), jax.ShapeDtypeStruct(ds.shape, ds.dtype)),
        in_specs=[pl.BlockSpec(memory_space=pltpu.SMEM)] + [any_spec] * (2 * n + 2) + [vm] + [any_spec] * 3,
        out_specs=(vm, any_spec),
        scratch_shapes=[
            pltpu.VMEM((2, D, D), BF16),
            pltpu.VMEM((rows, D), BF16),
            pltpu.VMEM((2, rows, D), BF16),
            pltpu.VMEM((2, rows, D), F32),
            pltpu.VMEM((rows, D), F32),
            pltpu.VMEM((2, rows, D), BF16),
            pltpu.SemaphoreType.DMA((2, NZ)),
            pltpu.SemaphoreType.DMA((3, 2)),
            pltpu.SemaphoreType.DMA((2,)),
        ],
        input_output_aliases={2 * n + 6: 1},
        compiler_params=pltpu.CompilerParams(vmem_limit_bytes=VMEM_LIMIT),
        cost_estimate=pl.CostEstimate(flops=4 * rows * D * D, bytes_accessed=4 * D * D, transcendentals=2 * rows * D),
        name="backward_tick",
    )(ctl, *near, *far, cot, recv, vec, xs, ls, ds)

AXES = ("y", "xl", "z", "xh", "c")
MICRO = 2
STAGES = 4

FIRST_DECAY = 0.9
SECOND_DECAY = 0.999
STEP_SIZE = 0.01
EPSILON = 1e-08
FIRST_CORRECTION = 1.0 - 0.9**10
SECOND_CORRECTION = 1.0 - 0.999**10


def shift_x(v, by):
    place = lambda x: (x & 1) * 2 + (x >> 1)
    return lax.ppermute(v, ("xl", "xh"), [(place(x), place((x + by) % 4)) for x in range(4)])


def shift_z(v, by):
    return lax.ppermute(v, "z", [(z, (z + by) % 8) for z in range(8)])


def swap_core(v):
    return lax.ppermute(v, "c", [(0, 1), (1, 0)])


def swap_pair(v):
    return lax.ppermute(v, "xl", [(0, 1), (1, 0)])


def swap_cross(v):
    return lax.ppermute(v, ("y", "xl"), [(3, 4), (4, 3)])


def ring_gather(v, shift, steps):
    right = left = v
    out = []
    for _ in range(1, steps):
        right, left = shift(right, 1), shift(left, -1)
        out += [right, left]
    half = v.shape[0] // 2
    return out + [shift(right[:half], 1), shift(left[half:], -1)]


def gather_plane(rows):
    a = rows[:32][None]
    b = rows[32:].reshape(2, 16, D)
    near_x = [a, shift_x(a, 1), shift_x(a, -1), shift_x(a, 2)]
    along_z = jnp.concatenate([b] + ring_gather(b, shift_z, 4), axis=0).reshape(8, 32, D)
    heads = jnp.concatenate(near_x, axis=0)
    return [heads] + ring_gather(heads, shift_z, 4) + [along_z] + ring_gather(along_z, shift_x, 2)


def add_rounded(a, b):
    return (a.astype(F32) + b.astype(F32)).astype(BF16)


def ring_reduce(chunks, shift, steps):
    half = chunks.shape[1] // 2
    far = chunks[steps]
    right, left = shift(far[:half], 1), shift(far[half:], -1)
    for k in range(steps - 1, 0, -1):
        up, down = chunks[k], chunks[2 * steps - k]
        if k == steps - 1:
            right = jnp.concatenate([add_rounded(up[:half], right), up[half:]], axis=0)
            left = jnp.concatenate([down[:half], add_rounded(down[half:], left)], axis=0)
        else:
            right, left = add_rounded(up, right), add_rounded(down, left)
        right, left = shift(right, 1), shift(left, -1)
    return chunks[0].astype(F32) + right.astype(F32) + left.astype(F32)


def grad_kernel(at, ds, g1, g2):
    for parity in range(2):
        block = at[:, parity].reshape(2 * 2 * 64, at.shape[-1])
        for n in range(4):
            cols = pl.ds(n * 512, 512)
            part = jnp.dot(block, ds[parity, :, cols], preferred_element_type=F32).astype(BF16)
            part = part.reshape(2, 2, 2, 32, 512)
            for z in range(2):
                for i in range(2):
                    g1[z, 2 * i + parity, :, cols] = part[z, i, 0]
                    g2[2 * i + parity, z, :, cols] = part[z, i, 1]


def grad_call(at, ds):
    tokens = at.shape[-1]
    return pl.pallas_call(
        grad_kernel,
        grid=(4,),
        out_shape=(jax.ShapeDtypeStruct((8, 4, 32, D), BF16), jax.ShapeDtypeStruct((4, 8, 32, D), BF16)),
        in_specs=[
            pl.BlockSpec((2, 2, 2, 64, tokens), lambda i: (i, 0, 0, 0, 0)),
            pl.BlockSpec((2, tokens, D), lambda i: (0, 0, 0)),
        ],
        out_specs=(
            pl.BlockSpec((2, 4, 32, D), lambda i: (i, 0, 0, 0)),
            pl.BlockSpec((4, 2, 32, D), lambda i: (0, i, 0, 0)),
        ),
        compiler_params=pltpu.CompilerParams(vmem_limit_bytes=VMEM_LIMIT),
        cost_estimate=pl.CostEstimate(flops=4 * tokens * D * 1024, bytes_accessed=12 << 20, transcendentals=0),
        name="weight_grads",
    )(at, ds)


def rolled(v, axis, by, order=None):
    size = v.shape[axis]
    return lax.dynamic_slice_in_dim(jnp.concatenate([v, v], axis=axis), by, size, axis=axis)


def scatter_grads(xs, ds, x_me, z_me, core, xl):
    x_all = jnp.concatenate([xs, swap_core(xs)], axis=1)
    d_all = jnp.concatenate([ds, swap_core(ds)], axis=1)
    tokens = x_all.shape[1]
    at = jnp.swapaxes(x_all, 1, 2).reshape(2, 8, 2, 2, 64, tokens)
    at = lax.dynamic_index_in_dim(at, core, 3, keepdims=False)
    at = at.transpose(1, 2, 0, 3, 4).reshape(8, 4, 64, tokens)
    at = rolled(rolled(at, 0, z_me), 1, x_me)
    at = at.reshape(8, 2, 2, 64, tokens).swapaxes(1, 2)
    d_all = rolled(d_all, 0, xl)
    g1, g2 = grad_call(at, d_all)
    first = ring_reduce(g1, shift_z, 4).astype(BF16)
    second = ring_reduce(g2, shift_x, 2).astype(BF16)
    first = (
        first[0].astype(F32)
        + shift_x(first[1], 1).astype(F32)
        + shift_x(first[3], -1).astype(F32)
        + shift_x(first[2], 2).astype(F32)
    )
    second = ring_reduce(second.reshape(8, 2, 16, D), shift_z, 4).reshape(32, D)
    return jnp.concatenate([first, second], axis=0)


def pick(stacked, mask):
    shaped = mask.reshape((-1,) + (1,) * (stacked.ndim - 1))
    return jnp.sum(jnp.where(shaped, stacked, jnp.zeros_like(stacked)), axis=0)


def shards(master_old, first_old, second_old, layer_vectors, new_section, frozen, window_input, cotangent):
    y, xl, z_me, xh, core = (lax.axis_index(name) for name in AXES)
    section = y * 2 + xl
    x_me = xl + 2 * xh
    stay = new_section == section
    pair = new_section == jnp.bitwise_xor(section, 1)
    cross = jnp.where(section == 3, new_section == 4, (section == 4) & (new_section == 3))
    plane = stay | pair
    label = jnp.where(jnp.any(plane), jnp.sum(jnp.where(plane, new_section, 0)) & 1, xl)

    held = pick(master_old, plane).astype(BF16) + swap_cross(pick(master_old, cross).astype(BF16))
    near = gather_plane(held)
    far = [swap_core(m) for m in near]
    own_vec = pick(layer_vectors, plane) + swap_cross(pick(layer_vectors, cross))
    other_vec = swap_pair(own_vec)
    vec = jnp.where(label == 0, jnp.stack([own_vec, other_vec]), jnp.stack([other_vec, own_vec])).astype(F32)

    tokens = window_input.shape[0] // 2
    rows = tokens // MICRO
    xs = jnp.zeros((2, tokens, D), BF16)
    ls = jnp.zeros((2, tokens, D), F32)
    ds = jnp.zeros((2, tokens, D), BF16)
    ahead = behind = jnp.zeros((rows, D), BF16)

    def control(batch):
        active = (batch >= 0) & (batch < MICRO)
        slot = jnp.clip(batch, 0, MICRO - 1)
        parts = [active, y, slot, x_me, z_me, core, label, xl]
        return jnp.stack([jnp.asarray(p, jnp.int32) for p in parts])

    for tick in range(MICRO + 2 * STAGES - 2):
        f_stages = [s for s in range(STAGES) if 0 <= tick - s < MICRO]
        b_stages = [s for s in range(STAGES) if 0 <= tick - 2 * (STAGES - 1) + s < MICRO]
        if f_stages:
            act, xs, ls = forward_call(control(tick - y), near, far, window_input, ahead, vec, xs, ls)
            pairs = [(s, s + 1) for s in f_stages if s + 1 < STAGES]
            if pairs:
                ahead = lax.ppermute(act, "y", pairs)
        if b_stages:
            back, ds = backward_call(
                control(tick - 2 * (STAGES - 1) + y), near, far, cotangent, behind, vec, xs, ls, ds
            )
            pairs = [(s, s - 1) for s in b_stages if s > 0]
            if pairs:
                behind = lax.ppermute(back, "y", pairs)

    zero = (near[-1][0, 0, 0].astype(F32) * 0.0).astype(jnp.int32)
    late = new_section + zero
    states = (master_old, first_old, second_old)
    send = lambda mask: jnp.stack([pick(s, mask) for s in states])
    late_pair = late == jnp.bitwise_xor(section, 1)
    late_cross = jnp.where(section == 3, late == 4, (section == 4) & (late == 3))
    moved = swap_pair(send(late_pair)) + swap_cross(send(late_cross))
    master, first_state, second_state = (pick(s, stay) + moved[i] for i, s in enumerate(states))

    grad_rows = scatter_grads(xs, ds, x_me, z_me, core, xl)
    learning = lax.dynamic_index_in_dim(frozen, section, 0, keepdims=False) == 0
    first_next = FIRST_DECAY * first_state + (1.0 - FIRST_DECAY) * grad_rows
    second_next = SECOND_DECAY * second_state + (1.0 - SECOND_DECAY) * grad_rows * grad_rows
    stepped = master - STEP_SIZE * (first_next / FIRST_CORRECTION) / (
        jnp.sqrt(second_next / SECOND_CORRECTION) + EPSILON
    )
    master_new = jnp.where(learning, stepped, master)
    first_new = jnp.where(learning, first_next, first_state)
    second_new = jnp.where(learning, second_next, second_state)
    return (master_new[None], first_new[None], second_new[None])


def solution(mesh):
    fine = jax.sharding.Mesh(mesh.devices.reshape(4, 2, 8, 2, 2), AXES)
    sec, rep = ("y", "xl"), ("z", "xh", "c")
    rows = P(sec, rep, None)
    in_specs = (rows, rows, rows, P(sec, None, None), P(sec), P(), P(rep, None), P(rep, None))
    return jax.shard_map(shards, mesh=fine, in_specs=in_specs, out_specs=(rows, rows, rows), check_vma=False)
```

time: 826 us -> 527 us (0.64)
  the two profiles are of different devices: /device:TPU:6 before, /device:TPU:16 now
where the time goes in v1:
time: 527 us; the launch traced here: 519 us
  waiting for transfers between devices  210 us (40%)
  starting transfers between devices  133 us (25%)
  Pallas kernels  100 us (19%)
  local copies, waits for them, and re-layouts  43.1 us (8%)
  other arithmetic  27.1 us (5%)
    ppermute x32, waiting for transfers between devices, shift_z(): return lax.ppermute(v, 'z', [(z, (z + by) % 8) for z in range(8)])  80.5 us
    ppermute x14, waiting for transfers between devices, shift_x(): lax.ppermute(v, ('xl', 'xh'), [(place(x), place((x + by) % 4)) for x in r...  59.7 us
    ppermute x32, starting transfers between devices, shift_z(): return lax.ppermute(v, 'z', [(z, (z + by) % 8) for z in range(8)])  53 us
    pallas_call x5, Pallas kernels, backward_call(): pl.pallas_call(functools.partial(backward_kernel, n, rows), out_shape=(ja...  52.8 us
    pallas_call x5, Pallas kernels, forward_call(): pl.pallas_call(functools.partial(forward_kernel, n, rows), out_shape=(jax...  42.5 us
    ppermute x4, waiting for transfers between devices, shards(): ahead = lax.ppermute(act, 'y', pairs)  38.8 us
    ppermute x3, starting transfers between devices, swap_cross(): return lax.ppermute(v, ('y', 'xl'), [(3, 4), (4, 3)])  33.6 us
    ppermute x14, starting transfers between devices, shift_x(): lax.ppermute(v, ('xl', 'xh'), [(place(x), place((x + by) % 4)) for x in r...  30.9 us
  transfers between devices with their start and end apart: 75, of which 28 were waited for; matrix products, arithmetic and copies ran while one was open for 7% of the time, Pallas kernels for 6%

profile of v1, /device:TPU:16, one launch (start us, length us, event | category | flops | bytes accessed | tf_op | source)
XLA Modules:
  0.0 518.7 jit_solution(8360808790882402317)
XLA Ops:
  21.6 5.9 %collective-permute-start.2 = (bf16[2,16,2048]{2,1,0:T(8,128)(2,1)S(1)}, bf16[2,16,2048]{2,1,0:T(8,128)(2,1)S(1)}, u32[]{:S(2)}, u32[]{:S(2)}) collective-permute-start(bf16[2,16,2048]{2,1,0:T(8,128)(2,1)S(1)} %bitcast.165), channel_id=1, source_target_pairs={{0,28},{4,0},{8,4},{12,8},{16,12},{20,16},{24,20},{28,24},{1,29},{... | collective-permute-start | bytes 393224 | tf_op jit(solution)/shard_map/ppermute | solution.py:283
  27.7 5.7 %collective-permute-start.17 = (bf16[4,32,2048]{2,1,0:T(8,128)(2,1)S(1)}, bf16[4,32,2048]{2,1,0:T(8,128)(2,1)S(1)}, u32[]{:S(2)}, u32[]{:S(2)}) collective-permute-start(bf16[4,32,2048]{2,1,0:T(8,128)(2,1)S(1)} %pad_maximum_fusion.4.refs_0_), channel_id=1, source_target_pairs={{0,28},{4,0},{8,4},{12,8},{16,12},{20,16},{24,20},{28,24},{1,29},{... | collective-permute-start | bytes 1572872 | tf_op jit(solution)/shard_map/ppermute | solution.py:283
  36.7 8.3 %collective-permute-done.4 = bf16[2,16,2048]{2,1,0:T(8,128)(2,1)S(1)} collective-permute-done((bf16[2,16,2048]{2,1,0:T(8,128)(2,1)S(1)}, bf16[2,16,2048]{2,1,0:T(8,128)(2,1)S(1)}, u32[]{:S(2)}, u32[]{:S(2)}) %collective-permute-start.4) | collective-permute-done | bytes 131104 | tf_op jit(solution)/shard_map/ppermute | solution.py:283
  55.7 5.4 %collective-permute-done.7 = bf16[1,16,2048]{2,1,0:T(8,128)(2,1)S(1)} collective-permute-done((bf16[1,16,2048]{2,1,0:T(8,128)(2,1)S(1)}, bf16[1,16,2048]{2,1,0:T(8,128)(2,1)S(1)}, u32[]{:S(2)}, u32[]{:S(2)}) %collective-permute-start.7) | collective-permute-done | bytes 65568 | tf_op jit(solution)/shard_map/ppermute | solution.py:283
  66.8 12.2 %collective-permute-done.19.refs_4_ = bf16[4,32,2048]{2,1,0:T(8,128)(2,1)S(1)} collective-permute-done((bf16[4,32,2048]{2,1,0:T(8,128)(2,1)S(1)}, bf16[4,32,2048]{2,1,0:T(8,128)(2,1)S(1)}, u32[]{:S(2)}, u32[]{:S(2)}) %collective-permute-start.19) | collective-permute-done | bytes 524320 | tf_op jit(solution)/shard_map/ppermute | solution.py:283
  82.3 10.3 %collective-permute-done.21.refs_6_ = bf16[4,32,2048]{2,1,0:T(8,128)(2,1)S(1)} collective-permute-done((bf16[4,32,2048]{2,1,0:T(8,128)(2,1)S(1)}, bf16[4,32,2048]{2,1,0:T(8,128)(2,1)S(1)}, u32[]{:S(2)}, u32[]{:S(2)}) %collective-permute-start.21) | collective-permute-done | bytes 524320 | tf_op jit(solution)/shard_map/ppermute | solution.py:283
  102.8 6.1 %collective-permute-done.23.refs_8_ = bf16[2,32,2048]{2,1,0:T(8,128)(2,1)S(1)} collective-permute-done((bf16[2,32,2048]{2,1,0:T(8,128)(2,1)S(1)}, bf16[2,32,2048]{2,1,0:T(8,128)(2,1)S(1)}, u32[]{:S(2)}, u32[]{:S(2)}) %collective-permute-start.23) | collective-permute-done | bytes 262176 | tf_op jit(solution)/shard_map/ppermute | solution.py:283
  132.4 31.3 %collective-permute-done.43.refs_29_ = bf16[64,2048]{1,0:T(8,128)(2,1)} collective-permute-done((bf16[64,2048]{1,0:T(8,128)(2,1)}, bf16[64,2048]{1,0:T(8,128)(2,1)}, u32[]{:S(2)}, u32[]{:S(2)}) %collective-permute-start.43) | collective-permute-done | bytes 262176 | tf_op jit(solution)/shard_map/ppermute | solution.py:439
  167.6 14.4 %forward_tick.7 = (bf16[64,2048]{1,0:T(8,128)(2,1)}, bf16[2,128,2048]{2,1,0:T(8,128)(2,1)}, f32[2,128,2048]{2,1,0:T(8,128)}) custom-call(s32[8]{0:T(128)S(1)} %stack.255.ctl, bf16[4,32,2048]{2,1,0:T(8,128)(2,1)S(1)} %pad_maximum_fusion.4.refs_0_, ...), custom_call_target="tpu_custom_call", output_to_operand_aliasing={{1}: (32, {}), {2}: (33, {})} | custom-call | flops 1073741824 | bytes 16777216 | tf_op jit(solution)/shard_map/forward_tick/pallas_call | solution.py:214
  184.1 7.5 %collective-permute-done.44.refs_29_ = bf16[64,2048]{1,0:T(8,128)(2,1)} collective-permute-done((bf16[64,2048]{1,0:T(8,128)(2,1)}, bf16[64,2048]{1,0:T(8,128)(2,1)}, u32[]{:S(2)}, u32[]{:S(2)}) %collective-permute-start.44) | collective-permute-done | bytes 262176 | tf_op jit(solution)/shard_map/ppermute | solution.py:439
  195.5 13.8 %forward_tick.8 = (bf16[64,2048]{1,0:T(8,128)(2,1)}, bf16[2,128,2048]{2,1,0:T(8,128)(2,1)}, f32[2,128,2048]{2,1,0:T(8,128)}) custom-call(s32[8]{0:T(128)S(1)} %stack.251.ctl, bf16[4,32,2048]{2,1,0:T(8,128)(2,1)S(1)} %pad_maximum_fusion.4.refs_0_, ...), custom_call_target="tpu_custom_call", output_to_operand_aliasing={{1}: (32, {}), {2}: (33, {})} | custom-call | flops 1073741824 | bytes 16777216 | tf_op jit(solution)/shard_map/forward_tick/pallas_call | solution.py:214
  220.3 11.4 %forward_tick.9 = (bf16[64,2048]{1,0:T(8,128)(2,1)}, bf16[2,128,2048]{2,1,0:T(8,128)(2,1)}, f32[2,128,2048]{2,1,0:T(8,128)}) custom-call(s32[8]{0:T(128)S(1)} %stack.247.ctl, bf16[4,32,2048]{2,1,0:T(8,128)(2,1)S(1)} %pad_maximum_fusion.4.refs_0_, ...), custom_call_target="tpu_custom_call", output_to_operand_aliasing={{1}: (32, {}), {2}: (33, {})} | custom-call | flops 1073741824 | bytes 16777216 | tf_op jit(solution)/shard_map/forward_tick/pallas_call | solution.py:214
  231.7 7.0 %collective-permute-done.47.refs_29_ = bf16[64,2048]{1,0:T(8,128)(2,1)} collective-permute-done((bf16[64,2048]{1,0:T(8,128)(2,1)}, bf16[64,2048]{1,0:T(8,128)(2,1)}, u32[]{:S(2)}, u32[]{:S(2)}) %collective-permute-start.47) | collective-permute-done | bytes 262176 | tf_op jit(solution)/shard_map/ppermute | solution.py:446
  238.7 20.0 %backward_tick.6 = (bf16[64,2048]{1,0:T(8,128)(2,1)}, bf16[2,128,2048]{2,1,0:T(8,128)(2,1)}) custom-call(s32[8]{0:T(128)S(1)} %stack.283.ctl, bf16[4,32,2048]{2,1,0:T(8,128)(2,1)S(1)} %pad_maximum_fusion.4.refs_0_, bf16[4,32,2048]{2,1,0:T(8,128)(2,1)S(1)} %collective-permute-done.16.refs_1_, ...), custom_call_target="tpu_custom_call", output_to_operand_aliasing={{1}: (34, {})} | custom-call | flops 1073741824 | bytes 16777216 | tf_op jit(solution)/shard_map/backward_tick/pallas_call | solution.py:243
  260.7 18.5 %collective-permute-done.48.refs_29_ = bf16[64,2048]{1,0:T(8,128)(2,1)} collective-permute-done((bf16[64,2048]{1,0:T(8,128)(2,1)}, bf16[64,2048]{1,0:T(8,128)(2,1)}, u32[]{:S(2)}, u32[]{:S(2)}) %collective-permute-start.48) | collective-permute-done | bytes 262176 | tf_op jit(solution)/shard_map/ppermute | solution.py:446
  283.1 20.1 %backward_tick.7 = (bf16[64,2048]{1,0:T(8,128)(2,1)}, bf16[2,128,2048]{2,1,0:T(8,128)(2,1)}) custom-call(s32[8]{0:T(128)S(1)} %stack.279.ctl, bf16[4,32,2048]{2,1,0:T(8,128)(2,1)S(1)} %pad_maximum_fusion.4.refs_0_, bf16[4,32,2048]{2,1,0:T(8,128)(2,1)S(1)} %collective-permute-done.16.refs_1_, ...), custom_call_target="tpu_custom_call", output_to_operand_aliasing={{1}: (34, {})} | custom-call | flops 1073741824 | bytes 16777216 | tf_op jit(solution)/shard_map/backward_tick/pallas_call | solution.py:243
  316.2 10.4 %backward_tick.9 = (bf16[64,2048]{1,0:T(8,128)(2,1)}, bf16[2,128,2048]{2,1,0:T(8,128)(2,1)}) custom-call(s32[8]{0:T(128)S(1)} %stack.271.ctl, bf16[4,32,2048]{2,1,0:T(8,128)(2,1)S(1)} %pad_maximum_fusion.4.refs_0_, bf16[4,32,2048]{2,1,0:T(8,128)(2,1)S(1)} %collective-permute-done.16.refs_1_, ...), custom_call_target="tpu_custom_call", output_to_operand_aliasing={{1}: (34, {})} | custom-call | flops 1073741824 | bytes 16777216 | tf_op jit(solution)/shard_map/backward_tick/pallas_call | solution.py:243
  328.0 26.9 %collective-permute-start.12 = (f32[3,64,2048]{2,1,0:T(8,128)}, f32[3,64,2048]{2,1,0:T(8,128)}, u32[]{:S(2)}, u32[]{:S(2)}) collective-permute-start(f32[3,64,2048]{2,1,0:T(8,128)} %pad_maximum_fusion.1), channel_id=1, source_target_pairs={{96,128},{128,96},{97,129},{129,97},{98,130},{130,98},{99,131},{13... | collective-permute-start | bytes 4718600 | tf_op jit(solution)/shard_map/ppermute | solution.py:295
  364.4 4.9 weight_grads.1
  386.9 47.3 %collective-permute-done.63 = bf16[4,32,2048]{2,1,0:T(8,128)(2,1)S(1)} collective-permute-done((bf16[4,32,2048]{2,1,0:T(8,128)(2,1)S(1)}, bf16[4,32,2048]{2,1,0:T(8,128)(2,1)S(1)}, u32[]{:S(2)}, u32[]{:S(2)}) %collective-permute-start.63) | collective-permute-done | bytes 524320 | tf_op jit(solution)/shard_map/ppermute | solution.py:279
  436.0 5.6 %collective-permute-start.66 = (bf16[8,32,2048]{2,1,0:T(8,128)(2,1)S(1)}, bf16[8,32,2048]{2,1,0:T(8,128)(2,1)S(1)}, u32[]{:S(2)}, u32[]{:S(2)}) collective-permute-start(bf16[8,32,2048]{2,1,0:T(8,128)(2,1)S(1)} %pad_maximum_fusion.3), channel_id=1, source_target_pairs={{0,34},{32,0},{2,32},{34,2},{1,35},{33,1},{3,33},{35,3},{4,38},{36... | collective-permute-start | bytes 3145736 | tf_op jit(solution)/shard_map/ppermute | solution.py:279
  441.7 7.3 %collective-permute-done.53 = bf16[4,32,2048]{2,1,0:T(8,128)(2,1)S(1)} collective-permute-done((bf16[4,32,2048]{2,1,0:T(8,128)(2,1)S(1)}, bf16[4,32,2048]{2,1,0:T(8,128)(2,1)S(1)}, u32[]{:S(2)}, u32[]{:S(2)}) %collective-permute-start.53) | collective-permute-done | bytes 524320 | tf_op jit(solution)/shard_map/ppermute | solution.py:283
  457.0 10.4 %collective-permute-done.54 = bf16[4,32,2048]{2,1,0:T(8,128)(2,1)} collective-permute-done((bf16[4,32,2048]{2,1,0:T(8,128)(2,1)}, bf16[4,32,2048]{2,1,0:T(8,128)(2,1)}, u32[]{:S(2)}, u32[]{:S(2)}) %collective-permute-start.54) | collective-permute-done | bytes 524320 | tf_op jit(solution)/shard_map/ppermute | solution.py:283
  502.1 5.7 %collective-permute-done.59 = bf16[4,32,2048]{2,1,0:T(8,128)(2,1)S(1)} collective-permute-done((bf16[4,32,2048]{2,1,0:T(8,128)(2,1)S(1)}, bf16[4,32,2048]{2,1,0:T(8,128)(2,1)S(1)}, u32[]{:S(2)}, u32[]{:S(2)}) %collective-permute-start.59) | collective-permute-done | bytes 524320 | tf_op jit(solution)/shard_map/ppermute | solution.py:283
  (325 shorter events, 197.5 us)
Async XLA Ops:
  16.2 48.4 %collective-permute-start.41 = (bf16[3,2048]{1,0:T(4,128)(2,1)S(1)}, bf16[3,2048]{1,0:T(4,128)(2,1)S(1)}, u32[]{:S(2)}, u32[]{:S(2)}) collective-permute-start(bf16[3,2048]{1,0:T(4,128)(2,1)S(1)} %add.150), channel_id=1, source_target_pairs={{0,32},{32,0},{1,33},{33,1},{2,34},{34,2},{3,35},{35,3},{4,36},{36... | collective-permute-start | bytes 36872 | tf_op jit(solution)/shard_map/ppermute | solution.py:291
  27.7 37.0 %collective-permute-start.17 = (bf16[4,32,2048]{2,1,0:T(8,128)(2,1)S(1)}, bf16[4,32,2048]{2,1,0:T(8,128)(2,1)S(1)}, u32[]{:S(2)}, u32[]{:S(2)}) collective-permute-start(bf16[4,32,2048]{2,1,0:T(8,128)(2,1)S(1)} %pad_maximum_fusion.4.refs_0_), channel_id=1, source_target_pairs={{0,28},{4,0},{8,4},{12,8},{16,12},{20,16},{24,20},{28,24},{1,29},{... | collective-permute-start | bytes 1572872 | tf_op jit(solution)/shard_map/ppermute | solution.py:283
  33.4 31.4 %collective-permute-start.16 = (bf16[4,32,2048]{2,1,0:T(8,128)(2,1)S(1)}, bf16[4,32,2048]{2,1,0:T(8,128)(2,1)S(1)}, u32[]{:S(2)}, u32[]{:S(2)}) collective-permute-start(bf16[4,32,2048]{2,1,0:T(8,128)(2,1)S(1)} %pad_maximum_fusion.4.refs_0_), channel_id=1, source_target_pairs={{0,4},{4,8},{8,12},{12,16},{16,20},{20,24},{24,28},{28,0},{1,5},{5... | collective-permute-start | bytes 1572872 | tf_op jit(solution)/shard_map/ppermute | solution.py:283
  61.2 20.6 %collective-permute-start.24 = (bf16[8,32,2048]{2,1,0:T(8,128)(2,1)S(1)}, bf16[8,32,2048]{2,1,0:T(8,128)(2,1)}, u32[]{:S(2)}, u32[]{:S(2)}) collective-permute-start(bf16[8,32,2048]{2,1,0:T(8,128)(2,1)S(1)} %bitcast.137), channel_id=1, source_target_pairs={{0,32},{32,2},{2,34},{34,0},{1,33},{33,3},{3,35},{35,1},{4,36},{36... | collective-permute-start | bytes 3145736 | tf_op jit(solution)/shard_map/ppermute | solution.py:279
  61.3 20.5 %collective-permute-start.9 = (bf16[8,32,2048]{2,1,0:T(8,128)(2,1)S(1)}, bf16[8,32,2048]{2,1,0:T(8,128)(2,1)}, u32[]{:S(2)}, u32[]{:S(2)}) collective-permute-start(bf16[8,32,2048]{2,1,0:T(8,128)(2,1)S(1)} %bitcast.138), channel_id=1, source_target_pairs={{0,34},{32,0},{2,32},{34,2},{1,35},{33,1},{3,33},{35,3},{4,38},{36... | collective-permute-start | bytes 3145736 | tf_op jit(solution)/shard_map/ppermute | solution.py:279
  64.8 15.7 %collective-permute-start.18 = (bf16[4,32,2048]{2,1,0:T(8,128)(2,1)S(1)}, bf16[4,32,2048]{2,1,0:T(8,128)(2,1)S(1)}, u32[]{:S(2)}, u32[]{:S(2)}) collective-permute-start(bf16[4,32,2048]{2,1,0:T(8,128)(2,1)S(1)} %collective-permute-done.16.refs_1_), channel_id=1, source_target_pairs={{0,4},{4,8},{8,12},{12,16},{16,20},{20,24},{24,28},{28,0},{1,5},{5... | collective-permute-start | bytes 1572872 | tf_op jit(solution)/shard_map/ppermute | solution.py:283
  66.8 34.0 %collective-permute-start.35 = (bf16[8,32,2048]{2,1,0:T(8,128)(2,1)S(1)}, bf16[8,32,2048]{2,1,0:T(8,128)(2,1)S(1)}, u32[]{:S(2)}, u32[]{:S(2)}) collective-permute-start(bf16[8,32,2048]{2,1,0:T(8,128)(2,1)S(1)} %bitcast.139), channel_id=1, source_target_pairs={{0,1},{1,0},{2,3},{3,2},{4,5},{5,4},{6,7},{7,6},{8,9},{9,8},{10,11... | collective-permute-start | bytes 3145736 | tf_op jit(solution)/shard_map/ppermute | solution.py:287
  81.8 15.7 %collective-permute-start.27 = (bf16[4,32,2048]{2,1,0:T(8,128)(2,1)S(1)}, bf16[4,32,2048]{2,1,0:T(8,128)(2,1)S(1)}, u32[]{:S(2)}, u32[]{:S(2)}) collective-permute-start(bf16[4,32,2048]{2,1,0:T(8,128)(2,1)S(1)} %collective-permute-done.16.refs_1_), channel_id=1, source_target_pairs={{0,1},{1,0},{2,3},{3,2},{4,5},{5,4},{6,7},{7,6},{8,9},{9,8},{10,11... | collective-permute-start | bytes 1572872 | tf_op jit(solution)/shard_map/ppermute | solution.py:287
  97.5 15.7 %collective-permute-start.25 = (bf16[4,32,2048]{2,1,0:T(8,128)(2,1)S(1)}, bf16[4,32,2048]{2,1,0:T(8,128)(2,1)}, u32[]{:S(2)}, u32[]{:S(2)}) collective-permute-start(bf16[4,32,2048]{2,1,0:T(8,128)(2,1)S(1)} %slice.267), channel_id=1, source_target_pairs={{0,32},{32,2},{2,34},{34,0},{1,33},{33,3},{3,35},{35,1},{4,36},{36... | collective-permute-start | bytes 1572872 | tf_op jit(solution)/shard_map/ppermute | solution.py:279
  102.8 17.1 %collective-permute-start.36 = (bf16[8,32,2048]{2,1,0:T(8,128)(2,1)}, bf16[8,32,2048]{2,1,0:T(8,128)(2,1)}, u32[]{:S(2)}, u32[]{:S(2)}) collective-permute-start(bf16[8,32,2048]{2,1,0:T(8,128)(2,1)} %collective-permute-done.24.refs_10_), channel_id=1, source_target_pairs={{0,1},{1,0},{2,3},{3,2},{4,5},{5,4},{6,7},{7,6},{8,9},{9,8},{10,11... | collective-permute-start | bytes 3145736 | tf_op jit(solution)/shard_map/ppermute | solution.py:287
  131.0 32.7 %collective-permute-start.43 = (bf16[64,2048]{1,0:T(8,128)(2,1)}, bf16[64,2048]{1,0:T(8,128)(2,1)}, u32[]{:S(2)}, u32[]{:S(2)}) collective-permute-start(bf16[64,2048]{1,0:T(8,128)(2,1)} %get-tuple-element.31), channel_id=1, source_target_pairs={{0,64},{64,128},{1,65},{65,129},{2,66},{66,130},{3,67},{67,131},{4... | collective-permute-start | bytes 786440 | tf_op jit(solution)/shard_map/ppermute | solution.py:439
  214.9 23.8 %collective-permute-start.47 = (bf16[64,2048]{1,0:T(8,128)(2,1)}, bf16[64,2048]{1,0:T(8,128)(2,1)}, u32[]{:S(2)}, u32[]{:S(2)}) collective-permute-start(bf16[64,2048]{1,0:T(8,128)(2,1)} %get-tuple-element.41), channel_id=1, source_target_pairs={{192,128},{193,129},{194,130},{195,131},{196,132},{197,133},{198,1... | collective-permute-start | bytes 786440 | tf_op jit(solution)/shard_map/ppermute | solution.py:446
  258.7 20.5 %collective-permute-start.48 = (bf16[64,2048]{1,0:T(8,128)(2,1)}, bf16[64,2048]{1,0:T(8,128)(2,1)}, u32[]{:S(2)}, u32[]{:S(2)}) collective-permute-start(bf16[64,2048]{1,0:T(8,128)(2,1)} %get-tuple-element.44), channel_id=1, source_target_pairs={{128,64},{192,128},{129,65},{193,129},{130,66},{194,130},{131,67},... | collective-permute-start | bytes 786440 | tf_op jit(solution)/shard_map/ppermute | solution.py:446
  307.3 48.8 %collective-permute-start.46 = (bf16[2,128,2048]{2,1,0:T(8,128)(2,1)}, bf16[2,128,2048]{2,1,0:T(8,128)(2,1)S(1)}, u32[]{:S(2)}, u32[]{:S(2)}) collective-permute-start(bf16[2,128,2048]{2,1,0:T(8,128)(2,1)} %get-tuple-element.40.refs_31_), channel_id=1, source_target_pairs={{0,1},{1,0},{2,3},{3,2},{4,5},{5,4},{6,7},{7,6},{8,9},{9,8},{10,11... | collective-permute-start | bytes 3145736 | tf_op jit(solution)/shard_map/ppermute | solution.py:287
  326.6 34.6 %collective-permute-start.51 = (bf16[2,128,2048]{2,1,0:T(8,128)(2,1)}, bf16[2,128,2048]{2,1,0:T(8,128)(2,1)S(1)}, u32[]{:S(2)}, u32[]{:S(2)}) collective-permute-start(bf16[2,128,2048]{2,1,0:T(8,128)(2,1)} %get-tuple-element.50), channel_id=1, source_target_pairs={{0,1},{1,0},{2,3},{3,2},{4,5},{5,4},{6,7},{7,6},{8,9},{9,8},{10,11... | collective-permute-start | bytes 3145736 | tf_op jit(solution)/shard_map/ppermute | solution.py:287
  328.0 125.5 %collective-permute-start.12 = (f32[3,64,2048]{2,1,0:T(8,128)}, f32[3,64,2048]{2,1,0:T(8,128)}, u32[]{:S(2)}, u32[]{:S(2)}) collective-permute-start(f32[3,64,2048]{2,1,0:T(8,128)} %pad_maximum_fusion.1), channel_id=1, source_target_pairs={{96,128},{128,96},{97,129},{129,97},{98,130},{130,98},{99,131},{13... | collective-permute-start | bytes 4718600 | tf_op jit(solution)/shard_map/ppermute | solution.py:295
  356.2 98.6 %collective-permute-start.11 = (f32[3,64,2048]{2,1,0:T(8,128)}, f32[3,64,2048]{2,1,0:T(8,128)}, u32[]{:S(2)}, u32[]{:S(2)}) collective-permute-start(f32[3,64,2048]{2,1,0:T(8,128)} %pad_maximum_fusion), channel_id=1, source_target_pairs={{0,32},{32,0},{1,33},{33,1},{2,34},{34,2},{3,35},{35,3},{4,36},{36... | collective-permute-start | bytes 4718600 | tf_op jit(solution)/shard_map/ppermute | solution.py:291
  375.5 58.8 %collective-permute-start.63 = (bf16[4,32,2048]{2,1,0:T(8,128)(2,1)S(1)}, bf16[4,32,2048]{2,1,0:T(8,128)(2,1)S(1)}, u32[]{:S(2)}, u32[]{:S(2)}) collective-permute-start(bf16[4,32,2048]{2,1,0:T(8,128)(2,1)S(1)} %get-tuple-element.83), channel_id=1, source_target_pairs={{0,32},{32,2},{2,34},{34,0},{1,33},{33,3},{3,35},{35,1},{4,36},{36... | collective-permute-start | bytes 1572872 | tf_op jit(solution)/shard_map/ppermute | solution.py:279
  380.2 54.1 %collective-permute-start.65 = (bf16[4,32,2048]{2,1,0:T(8,128)(2,1)S(1)}, bf16[4,32,2048]{2,1,0:T(8,128)(2,1)S(1)}, u32[]{:S(2)}, u32[]{:S(2)}) collective-permute-start(bf16[4,32,2048]{2,1,0:T(8,128)(2,1)S(1)} %get-tuple-element.84), channel_id=1, source_target_pairs={{0,34},{32,0},{2,32},{34,2},{1,35},{33,1},{3,33},{35,3},{4,38},{36... | collective-permute-start | bytes 1572872 | tf_op jit(solution)/shard_map/ppermute | solution.py:279
  386.9 70.1 %collective-permute-start.57 = (bf16[4,32,2048]{2,1,0:T(8,128)(2,1)}, bf16[4,32,2048]{2,1,0:T(8,128)(2,1)}, u32[]{:S(2)}, u32[]{:S(2)}) collective-permute-start(bf16[4,32,2048]{2,1,0:T(8,128)(2,1)} %pad_maximum_fusion.6), channel_id=1, source_target_pairs={{0,28},{4,0},{8,4},{12,8},{16,12},{20,16},{24,20},{28,24},{1,29},{... | collective-permute-start | bytes 1572872 | tf_op jit(solution)/shard_map/ppermute | solution.py:283
  436.0 36.3 %collective-permute-start.66 = (bf16[8,32,2048]{2,1,0:T(8,128)(2,1)S(1)}, bf16[8,32,2048]{2,1,0:T(8,128)(2,1)S(1)}, u32[]{:S(2)}, u32[]{:S(2)}) collective-permute-start(bf16[8,32,2048]{2,1,0:T(8,128)(2,1)S(1)} %pad_maximum_fusion.3), channel_id=1, source_target_pairs={{0,34},{32,0},{2,32},{34,2},{1,35},{33,1},{3,33},{35,3},{4,38},{36... | collective-permute-start | bytes 3145736 | tf_op jit(solution)/shard_map/ppermute | solution.py:279
  449.1 27.6 %collective-permute-start.64 = (bf16[8,32,2048]{2,1,0:T(8,128)(2,1)S(1)}, bf16[8,32,2048]{2,1,0:T(8,128)(2,1)}, u32[]{:S(2)}, u32[]{:S(2)}) collective-permute-start(bf16[8,32,2048]{2,1,0:T(8,128)(2,1)S(1)} %pad_maximum_fusion.2), channel_id=1, source_target_pairs={{0,32},{32,2},{2,34},{34,0},{1,33},{33,3},{3,35},{35,1},{4,36},{36... | collective-permute-start | bytes 3145736 | tf_op jit(solution)/shard_map/ppermute | solution.py:279
  469.0 33.1 %collective-permute-start.55 = (bf16[4,32,2048]{2,1,0:T(8,128)(2,1)S(1)}, bf16[4,32,2048]{2,1,0:T(8,128)(2,1)S(1)}, u32[]{:S(2)}, u32[]{:S(2)}) collective-permute-start(bf16[4,32,2048]{2,1,0:T(8,128)(2,1)S(1)} %get-tuple-element.73), channel_id=1, source_target_pairs={{0,4},{4,8},{8,12},{12,16},{16,20},{20,24},{24,28},{28,0},{1,5},{5... | collective-permute-start | bytes 1572872 | tf_op jit(solution)/shard_map/ppermute | solution.py:283
  469.1 25.0 %collective-permute-start.58 = (bf16[4,32,2048]{2,1,0:T(8,128)(2,1)S(1)}, bf16[4,32,2048]{2,1,0:T(8,128)(2,1)S(1)}, u32[]{:S(2)}, u32[]{:S(2)}) collective-permute-start(bf16[4,32,2048]{2,1,0:T(8,128)(2,1)S(1)} %get-tuple-element.74), channel_id=1, source_target_pairs={{0,28},{4,0},{8,4},{12,8},{16,12},{20,16},{24,20},{28,24},{1,29},{... | collective-permute-start | bytes 1572872 | tf_op jit(solution)/shard_map/ppermute | solution.py:283
  (105 other events, 839.8 us)

commit v2 on v1

v2 whole, which is shorter than its diff:
```python
import functools
import jax
import jax.numpy as jnp
from jax import lax
from jax.experimental import pallas as pl
from jax.experimental.pallas import tpu as pltpu
from jax.sharding import PartitionSpec as P

BF16 = jnp.bfloat16
F32 = jnp.float32
D = 2048
NZ = 8
VMEM_LIMIT = 60 * 1024 * 1024
GELU_K = 0.7978845608028654


def weight_copies(near, far, w_scr, sems, z_me, x_me, core):
    copies = ([], [])
    for msgs, owner in ((near, core), (far, 1 - core)):
        head, tail = msgs[:9], msgs[9:]
        for dx, ref, zs in ((0, 0, 0), (-1, 1, 0), (1, 2, 0), (2, 3, 0), (2, 4, 4)):
            xh = lax.rem(x_me + dx + 4, 4) // 2
            count = 8 if ref < 3 else 4
            dst = w_scr.at[dx % 2, pl.ds(zs, count), xh, owner, pl.ds(32, 32), :]
            copies[dx % 2].append(pltpu.make_async_copy(tail[ref], dst, sems.at[dx % 2, NZ]))
    for slot in range(2):
        for at, dz in enumerate((0, -1, 1, -2, 2, -3, 3, 4)):
            z = lax.rem(z_me + dz + 8, 8)
            for msgs, owner in ((near, core), (far, 1 - core)):
                src = msgs[at].at[slot] if at < 7 else msgs[7 + slot].at[0]
                dst = w_scr.at[slot, z, :, owner, pl.ds(0, 32), :]
                copies[slot].append(pltpu.make_async_copy(src, dst, sems.at[slot, dz % 8]))
    return copies


def gelu_parts(u):
    square = u * u
    t = jnp.tanh(GELU_K * u * (1.0 + 0.044715 * square))
    return 0.5 * u * (1.0 + t), t, square


def gelu_slope(u, t, square):
    return 0.5 * (1.0 + t) + 0.5 * u * (1.0 - t * t) * (GELU_K * (1.0 + 3 * 0.044715 * square))


def norm_parts(z):
    center = z - jnp.mean(z, axis=-1, keepdims=True)
    spread = jnp.mean(center * center, axis=-1, keepdims=True)
    return center, lax.rsqrt(spread + 1e-5)


def issue(groups, first):
    def start(slot):
        for copy in groups[slot]:
            copy.start()

    @pl.when(first == 0)
    def _():
        start(0)
        start(1)

    @pl.when(first == 1)
    def _():
        start(1)
        start(0)


def wait_tails(w_scr, sems, slot):
    rows = w_scr.at[slot, :, :, :, pl.ds(32, 32), :]
    pltpu.make_async_copy(rows, rows, sems.at[slot, NZ]).wait()


def wait_heads(w_scr, sems, slot, k, z):
    rows = w_scr.at[slot, z, :, :, pl.ds(0, 32), :]
    pltpu.make_async_copy(rows, rows, sems.at[slot, k]).wait()


def forward_kernel(n_msgs, rows, ctl, *refs):
    near, far = refs[:n_msgs], refs[n_msgs:2 * n_msgs]
    window, recv, vec_in, xs_in, ls_in, act, xs, ls, w_scr, x_scr, lin_scr, vec, act_scr, sems, sem_x, sem_v, sem_o = refs[2 * n_msgs:]
    del xs_in, ls_in
    active, stage, batch, x_me, z_me, core, first, xl = (ctl[i] for i in range(8))

    @pl.when(active == 1)
    def _():
        groups = weight_copies(near, far, w_scr, sems, z_me, x_me, core)
        per_half = window.shape[0] // 2
        at = pl.multiple_of(batch * rows, rows)

        @pl.when(stage == 0)
        def _():
            src = window.at[pl.ds(pl.multiple_of(xl * per_half + batch * rows, rows), rows), :]
            pltpu.make_async_copy(src, x_scr.at[0], sem_x).start()

        @pl.when(stage != 0)
        def _():
            pltpu.make_async_copy(recv, x_scr.at[0], sem_x).start()

        vec_copy = pltpu.make_async_copy(vec_in, vec, sem_v)
        vec_copy.start()
        issue(groups, first)
        vec_copy.wait()
        pltpu.make_async_copy(recv, x_scr.at[0], sem_x).wait()
        outs = []
        for layer in range(2):
            slot = first ^ layer
            lin_scr[layer] = jnp.broadcast_to(vec[layer, 0:1, :], (rows, D))
            wait_tails(w_scr, sems, slot)

            @pl.loop(0, NZ)
            def _(k):
                z = lax.rem(z_me + k, NZ)
                wait_heads(w_scr, sems, slot, k, z)
                cols = pl.ds(pl.multiple_of(z * 256, 256), 256)
                lin_scr[layer] += jnp.dot(
                    x_scr[layer, :, cols], w_scr[slot, z].reshape(256, D), preferred_element_type=F32
                )

            lin = lin_scr[layer]
            center, scale = norm_parts(x_scr[layer].astype(F32) + gelu_parts(lin)[0])
            y = (center * scale * vec[layer, 1:2, :] + vec[layer, 2:3, :]).astype(BF16)
            if layer == 0:
                x_scr[1] = y
            else:
                act_scr[...] = y
                outs.append(pltpu.make_async_copy(act_scr, act, sem_v))
                outs[-1].start()
            for src, dst, n in ((x_scr, xs, 0), (lin_scr, ls, 1)):
                copy = pltpu.make_async_copy(src.at[layer], dst.at[layer, pl.ds(at, rows), :], sem_o.at[layer, n])
                copy.start()
                outs.append(copy)
        for copy in outs:
            copy.wait()


def backward_kernel(n_msgs, rows, n_early, ctl, *refs):
    near, far = refs[:n_msgs], refs[n_msgs:2 * n_msgs]
    cot, recv, vec_in, xs, ls, ds_in = refs[2 * n_msgs:2 * n_msgs + 6]
    back, ds, w_scr, g_scr, x_scr, lin_scr, dz_scr, dl_scr, vec, back_scr, sems, sem_x, sem_v, sem_o = refs[2 * n_msgs + 6 + n_early:]
    del ds_in
    active, stage, batch, x_me, z_me, core, first, xl = (ctl[i] for i in range(8))

    @pl.when(active == 1)
    def _():
        groups = weight_copies(near, far, w_scr, sems, z_me, x_me, core)
        per_half = cot.shape[0] // 2
        at = pl.multiple_of(batch * rows, rows)

        @pl.when(stage == 3)
        def _():
            src = cot.at[pl.ds(pl.multiple_of(xl * per_half + batch * rows, rows), rows), :]
            pltpu.make_async_copy(src, g_scr, sem_x.at[2, 0]).start()

        @pl.when(stage != 3)
        def _():
            pltpu.make_async_copy(recv, g_scr, sem_x.at[2, 0]).start()

        loads = {}
        for layer in (1, 0):
            loads[layer] = (
                pltpu.make_async_copy(xs.at[layer, pl.ds(at, rows), :], x_scr.at[layer], sem_x.at[layer, 0]),
                pltpu.make_async_copy(ls.at[layer, pl.ds(at, rows), :], lin_scr.at[layer], sem_x.at[layer, 1]),
            )
            for copy in loads[layer]:
                copy.start()
        vec_copy = pltpu.make_async_copy(vec_in, vec, sem_v)
        vec_copy.start()
        issue(groups, 1 - first)
        vec_copy.wait()
        pltpu.make_async_copy(recv, g_scr, sem_x.at[2, 0]).wait()
        outs = []
        for layer in (1, 0):
            slot = first ^ layer
            for copy in loads[layer]:
                copy.wait()
            lin = lin_scr[layer]
            gated, t, square = gelu_parts(lin)
            center, scale = norm_parts(x_scr[layer].astype(F32) + gated)
            unit = center * scale
            g = g_scr[...].astype(F32) * vec[layer, 1:2, :]
            dz = scale * (g - jnp.mean(g, axis=-1, keepdims=True) - unit * jnp.mean(g * unit, axis=-1, keepdims=True))
            dz_scr[...] = dz
            dl_scr[layer] = (dz * gelu_slope(lin, t, square)).astype(BF16)
            copy = pltpu.make_async_copy(dl_scr.at[layer], ds.at[layer, pl.ds(at, rows), :], sem_o.at[layer])
            copy.start()
            outs.append(copy)
            wait_tails(w_scr, sems, slot)

            @pl.loop(0, NZ)
            def _(k):
                z = lax.rem(z_me + k, NZ)
                wait_heads(w_scr, sems, slot, k, z)
                cols = pl.ds(pl.multiple_of(z * 256, 256), 256)

                def step():
                    down = lax.dot_general(
                        dl_scr[layer], w_scr[slot, z].reshape(256, D), (((1,), (1,)), ((), ())), preferred_element_type=F32
                    )
                    y = (dz_scr[:, cols] + down).astype(BF16)
                    if layer == 1:
                        g_scr[:, cols] = y
                    else:
                        back_scr[:, cols] = y

                if layer == 1:
                    step()
                else:
                    pl.when(stage != 0)(step)
        outs.append(pltpu.make_async_copy(back_scr, back, sem_v))
        outs[-1].start()
        for copy in outs:
            copy.wait()


def forward_call(ctl, near, far, window, recv, vec, xs, ls):
    rows = recv.shape[0]
    n = len(near)
    any_spec = pl.BlockSpec(memory_space=pl.ANY)
    return pl.pallas_call(
        functools.partial(forward_kernel, n, rows),
        out_shape=(
            jax.ShapeDtypeStruct((rows, D), BF16),
            jax.ShapeDtypeStruct(xs.shape, xs.dtype),
            jax.ShapeDtypeStruct(ls.shape, ls.dtype),
        ),
        in_specs=[pl.BlockSpec(memory_space=pltpu.SMEM)] + [any_spec] * (2 * n + 5),
        out_specs=(any_spec, any_spec, any_spec),
        scratch_shapes=[
            pltpu.VMEM((2, 8, 2, 2, 64, D), BF16),
            pltpu.VMEM((2, rows, D), BF16),
            pltpu.VMEM((2, rows, D), F32),
            pltpu.VMEM(vec.shape, F32),
            pltpu.VMEM((rows, D), BF16),
            pltpu.SemaphoreType.DMA((2, NZ + 1)),
            pltpu.SemaphoreType.DMA,
            pltpu.SemaphoreType.DMA,
            pltpu.SemaphoreType.DMA((2, 2)),
        ],
        input_output_aliases={2 * n + 4: 1, 2 * n + 5: 2},
        compiler_params=pltpu.CompilerParams(vmem_limit_bytes=VMEM_LIMIT),
        cost_estimate=pl.CostEstimate(flops=4 * rows * D * D, bytes_accessed=4 * D * D, transcendentals=2 * rows * D),
        name="forward_tick",
    )(ctl, *near, *far, window, recv, vec, xs, ls)


def backward_call(ctl, near, far, cot, recv, vec, xs, ls, ds, early=()):
    rows = recv.shape[0]
    n = len(near)
    any_spec = pl.BlockSpec(memory_space=pl.ANY)
    return pl.pallas_call(
        functools.partial(backward_kernel, n, rows, len(early)),
        out_shape=(jax.ShapeDtypeStruct((rows, D), BF16), jax.ShapeDtypeStruct(ds.shape, ds.dtype)),
        in_specs=[pl.BlockSpec(memory_space=pltpu.SMEM)] + [any_spec] * (2 * n + 6 + len(early)),
        out_specs=(any_spec, any_spec),
        scratch_shapes=[
            pltpu.VMEM((2, 8, 2, 2, 64, D), BF16),
            pltpu.VMEM((rows, D), BF16),
            pltpu.VMEM((2, rows, D), BF16),
            pltpu.VMEM((2, rows, D), F32),
            pltpu.VMEM((rows, D), F32),
            pltpu.VMEM((2, rows, D), BF16),
            pltpu.VMEM(vec.shape, F32),
            pltpu.VMEM((rows, D), BF16),
            pltpu.SemaphoreType.DMA((2, NZ + 1)),
            pltpu.SemaphoreType.DMA((3, 2)),
            pltpu.SemaphoreType.DMA,
            pltpu.SemaphoreType.DMA((2,)),
        ],
        input_output_aliases={2 * n + 6: 1},
        compiler_params=pltpu.CompilerParams(vmem_limit_bytes=VMEM_LIMIT),
        cost_estimate=pl.CostEstimate(flops=4 * rows * D * D, bytes_accessed=4 * D * D, transcendentals=2 * rows * D),
        name="backward_tick",
    )(ctl, *near, *far, cot, recv, vec, xs, ls, ds, *early)

AXES = ("y", "xl", "z", "xh", "c")
MICRO = 2
STAGES = 4

FIRST_DECAY = 0.9
SECOND_DECAY = 0.999
STEP_SIZE = 0.01
EPSILON = 1e-08
FIRST_CORRECTION = 1.0 - 0.9**10
SECOND_CORRECTION = 1.0 - 0.999**10


def shift_x(v, by):
    place = lambda x: (x & 1) * 2 + (x >> 1)
    return lax.ppermute(v, ("xl", "xh"), [(place(x), place((x + by) % 4)) for x in range(4)])


def shift_z(v, by):
    return lax.ppermute(v, "z", [(z, (z + by) % 8) for z in range(8)])


def swap_core(v):
    return lax.ppermute(v, "c", [(0, 1), (1, 0)])


def swap_pair(v):
    return lax.ppermute(v, "xl", [(0, 1), (1, 0)])


def swap_cross(v):
    return lax.ppermute(v, ("y", "xl"), [(3, 4), (4, 3)])


def ring_gather(v, shift, steps):
    right = left = v
    out = []
    for _ in range(1, steps):
        right, left = shift(right, 1), shift(left, -1)
        out += [right, left]
    half = v.shape[0] // 2
    return out + [shift(right[:half], 1), shift(left[half:], -1)]


def gather_plane(rows, x_me, xh):
    a, b = rows[:32], rows[32:]
    before, after, across = shift_x(a, 1), shift_x(a, -1), shift_x(a, 2)
    along_z = lax.all_gather(b, "z", axis=0)
    own_first, before_first = xh == 0, lax.rem(x_me + 3, 4) < 2
    heads = jnp.stack(
        [
            jnp.stack([jnp.where(own_first, a, across), jnp.where(own_first, across, a)]),
            jnp.stack([jnp.where(before_first, before, after), jnp.where(before_first, after, before)]),
        ]
    )
    return [heads] + ring_gather(heads, shift_z, 4) + [along_z] + ring_gather(along_z, shift_x, 2)


def add_rounded(a, b):
    return (a.astype(F32) + b.astype(F32)).astype(BF16)


def ring_reduce(chunks, shift, steps):
    half = chunks.shape[1] // 2
    far = chunks[steps]
    right, left = shift(far[:half], 1), shift(far[half:], -1)
    for k in range(steps - 1, 0, -1):
        up, down = chunks[k], chunks[2 * steps - k]
        if k == steps - 1:
            right = jnp.concatenate([add_rounded(up[:half], right), up[half:]], axis=0)
            left = jnp.concatenate([down[:half], add_rounded(down[half:], left)], axis=0)
        else:
            right, left = add_rounded(up, right), add_rounded(down, left)
        right, left = shift(right, 1), shift(left, -1)
    return chunks[0].astype(F32) + right.astype(F32) + left.astype(F32)


def grad_kernel(n_parts, xt, *refs):
    parts, g, d_scr, sem = refs[:n_parts], refs[n_parts], refs[n_parts + 1], refs[n_parts + 2]
    size = parts[0].shape[0]
    for i, part in enumerate(parts):
        pltpu.make_async_copy(part, d_scr.at[pl.ds(i * size, size), :], sem).start()
    pltpu.make_async_copy(d_scr, d_scr, sem).wait()

    @pl.loop(0, D // 256)
    def _(n):
        cols = pl.ds(pl.multiple_of(n * 256, 256), 256)
        part = jnp.dot(xt[...], d_scr[:, cols], preferred_element_type=F32).astype(BF16)
        g[:, :, cols] = part.reshape(8, 64, 256)


def grad_call(xt, parts):
    tokens = xt.shape[1]
    return pl.pallas_call(
        functools.partial(grad_kernel, len(parts)),
        out_shape=jax.ShapeDtypeStruct((8, 64, D), BF16),
        in_specs=[pl.BlockSpec(memory_space=pltpu.VMEM)] + [pl.BlockSpec(memory_space=pl.ANY)] * len(parts),
        out_specs=pl.BlockSpec(memory_space=pltpu.VMEM),
        scratch_shapes=[pltpu.VMEM((tokens, D), BF16), pltpu.SemaphoreType.DMA],
        compiler_params=pltpu.CompilerParams(vmem_limit_bytes=VMEM_LIMIT),
        cost_estimate=pl.CostEstimate(flops=2 * tokens * D * 512, bytes_accessed=7 << 20, transcendentals=0),
        name="weight_grads",
    )(xt, *parts)


def rolled(v, axis, by):
    return lax.dynamic_slice_in_dim(jnp.concatenate([v, v], axis=axis), by, v.shape[axis], axis=axis)


def trade_inputs(xs, x_me, z_me, core):
    tokens = xs.shape[1]
    xt = jnp.swapaxes(xs, 1, 2).reshape(2, 8, 2, 2, 64, tokens)
    mine = lax.dynamic_index_in_dim(xt, core, 3, keepdims=False)
    theirs = lax.dynamic_index_in_dim(xt, 1 - core, 3, keepdims=False)
    both = jnp.concatenate([mine, swap_core(theirs)], axis=-1)

    def meant_for(step):
        x = lax.rem(x_me + step, 4)
        block = lax.dynamic_index_in_dim(both, x % 2, 0, keepdims=False)
        return lax.dynamic_index_in_dim(block, x // 2, 1, keepdims=False)

    blocks = [meant_for(0), shift_x(meant_for(1), 1), shift_x(meant_for(3), -1), shift_x(meant_for(2), 2)]
    return rolled(jnp.concatenate(blocks, axis=-1), 0, z_me).reshape(512, 8 * tokens)


def trade_slopes(ds, xl):
    own = lax.dynamic_index_in_dim(ds, xl, 0, keepdims=False)
    other = lax.dynamic_index_in_dim(ds, 1 - xl, 0, keepdims=False)
    parts = []
    for part in (own, shift_x(other, 1), shift_x(other, -1), shift_x(own, 2)):
        parts += [part, swap_core(part)]
    return parts


def plus_nothing(index, v):
    return index + (v[(0,) * v.ndim].astype(F32) * 0.0).astype(jnp.int32)


def pick(stacked, mask):
    shaped = mask.reshape((-1,) + (1,) * (stacked.ndim - 1))
    return jnp.sum(jnp.where(shaped, stacked, jnp.zeros_like(stacked)), axis=0)


def shards(master_old, first_old, second_old, layer_vectors, new_section, frozen, window_input, cotangent):
    y, xl, z_me, xh, core = (lax.axis_index(name) for name in AXES)
    section = y * 2 + xl
    x_me = xl + 2 * xh
    stay = new_section == section
    pair = new_section == jnp.bitwise_xor(section, 1)
    cross = jnp.where(section == 3, new_section == 4, (section == 4) & (new_section == 3))
    plane = stay | pair
    label = jnp.where(jnp.any(plane), jnp.sum(jnp.where(plane, new_section, 0)) & 1, xl)

    vec_pad = lambda mask: jnp.pad(pick(layer_vectors, mask), ((0, 13), (0, 0)))
    traded = swap_cross(jnp.concatenate([pick(master_old, cross).astype(BF16), vec_pad(cross)], axis=0))
    held = pick(master_old, plane).astype(BF16) + traded[:64]
    near = gather_plane(held, x_me, xh)
    far = [swap_core(m) for m in near]
    own_vec = pick(layer_vectors, plane) + traded[64:67]
    other_vec = swap_pair(own_vec)
    vec = jnp.where(label == 0, jnp.stack([own_vec, other_vec]), jnp.stack([other_vec, own_vec])).astype(F32)

    states = (master_old, first_old, second_old)
    send = lambda mask: jnp.stack([pick(s, mask) for s in states])
    soon, late = plus_nothing(new_section, near[0]), plus_nothing(new_section, near[-1])
    late_pair = late == jnp.bitwise_xor(section, 1)
    soon_cross = jnp.where(section == 3, soon == 4, (section == 4) & (soon == 3))
    moved = swap_pair(send(late_pair)) + swap_cross(send(soon_cross))

    tokens = window_input.shape[0] // 2
    rows = tokens // MICRO
    xs = jnp.zeros((2, tokens, D), BF16)
    ls = jnp.zeros((2, tokens, D), F32)
    ds = jnp.zeros((2, tokens, D), BF16)
    slopes = []
    ahead = behind = jnp.zeros((rows, D), BF16)

    def control(batch):
        active = (batch >= 0) & (batch < MICRO)
        slot = jnp.clip(batch, 0, MICRO - 1)
        parts = [active, y, slot, x_me, z_me, core, label, xl]
        return jnp.stack([jnp.asarray(p, jnp.int32) for p in parts])

    for tick in range(MICRO + 2 * STAGES - 2):
        f_stages = [s for s in range(STAGES) if 0 <= tick - s < MICRO]
        b_stages = [s for s in range(STAGES) if 0 <= tick - 2 * (STAGES - 1) + s < MICRO]
        if f_stages:
            act, xs, ls = forward_call(control(tick - y), near, far, window_input, ahead, vec, xs, ls)
            pairs = [(s, s + 1) for s in f_stages if s + 1 < STAGES]
            if pairs:
                ahead = lax.ppermute(act, "y", pairs)
        if b_stages:
            early = ()
            if tick == MICRO + 2 * STAGES - 3:
                xt = trade_inputs(xs, x_me, z_me, core)
                early = (xt, moved)
            back, ds = backward_call(
                control(tick - 2 * (STAGES - 1) + y), near, far, cotangent, behind, vec, xs, ls, ds, early
            )
            pairs = [(s, s - 1) for s in b_stages if s > 0]
            if pairs:
                behind = lax.ppermute(back, "y", pairs)
            done = tick - 2 * (STAGES - 1)
            if done >= 0:
                slopes.append(trade_slopes(ds[:, done * rows:(done + 1) * rows], xl))

    master, first_state, second_state = (pick(s, stay) + moved[i] for i, s in enumerate(states))

    parts = [slopes[m][i] for i in range(8) for m in range(MICRO)]
    grad_rows = ring_reduce(grad_call(xt, parts), shift_z, 4)
    learning = lax.dynamic_index_in_dim(frozen, section, 0, keepdims=False) == 0
    first_next = FIRST_DECAY * first_state + (1.0 - FIRST_DECAY) * grad_rows
    second_next = SECOND_DECAY * second_state + (1.0 - SECOND_DECAY) * grad_rows * grad_rows
    stepped = master - STEP_SIZE * (first_next / FIRST_CORRECTION) / (
        jnp.sqrt(second_next / SECOND_CORRECTION) + EPSILON
    )
    master_new = jnp.where(learning, stepped, master)
    first_new = jnp.where(learning, first_next, first_state)
    second_new = jnp.where(learning, second_next, second_state)
    return (master_new[None], first_new[None], second_new[None])


def solution(mesh):
    fine = jax.sharding.Mesh(mesh.devices.reshape(4, 2, 8, 2, 2), AXES)
    sec, rep = ("y", "xl"), ("z", "xh", "c")
    rows = P(sec, rep, None)
    in_specs = (rows, rows, rows, P(sec, None, None), P(sec), P(), P(rep, None), P(rep, None))
    return jax.shard_map(shards, mesh=fine, in_specs=in_specs, out_specs=(rows, rows, rows), check_vma=False)
```

time: 527 us -> 425 us (0.81)
  the two profiles are of different devices: /device:TPU:16 before, /device:TPU:6 now
where the time goes in v2:
time: 425 us; the launch traced here: 420 us
  waiting for transfers between devices  202 us (48%)
  starting transfers between devices  92.1 us (22%)
  Pallas kernels  52.3 us (12%)
  local copies, waits for them, and re-layouts  30.2 us (7%)
  other arithmetic  24.7 us (6%)
  between operations  18.9 us (4%)
    ppermute x4, waiting for transfers between devices, shards(): behind = lax.ppermute(back, 'y', pairs)  84 us
    ppermute x16, waiting for transfers between devices, shift_z(): return lax.ppermute(v, 'z', [(z, (z + by) % 8) for z in range(8)])  48.3 us
    ppermute x16, starting transfers between devices, shift_x(): lax.ppermute(v, ('xl', 'xh'), [(place(x), place((x + by) % 4)) for x in r...  41.6 us
    ppermute x16, waiting for transfers between devices, shift_x(): lax.ppermute(v, ('xl', 'xh'), [(place(x), place((x + by) % 4)) for x in r...  34.1 us
    all_gather x1, waiting for transfers between devices, gather_plane(): along_z = lax.all_gather(b, 'z', axis=0)  27.6 us
    ppermute x16, starting transfers between devices, shift_z(): return lax.ppermute(v, 'z', [(z, (z + by) % 8) for z in range(8)])  26.4 us
    pallas_call x5, Pallas kernels, forward_call(): pl.pallas_call(functools.partial(forward_kernel, n, rows), out_shape=(jax...  22.5 us
    pallas_call x5, Pallas kernels, backward_call(): pl.pallas_call(functools.partial(backward_kernel, n, rows, len(early)), o...  21.5 us
  transfers between devices with their start and end apart: 68, of which 23 were waited for; matrix products, arithmetic and copies ran while one was open for 8% of the time, Pallas kernels for 8%

profile of v2, /device:TPU:6, one launch (start us, length us, event | category | flops | bytes accessed | tf_op | source)
XLA Modules:
  0.0 420.4 jit_solution(17800007433795789451)
XLA Ops:
  16.0 4.4 %collective-permute-done.4 = bf16[32,2048]{1,0:T(8,128)(2,1)S(1)} collective-permute-done((bf16[32,2048]{1,0:T(8,128)(2,1)S(1)}, bf16[32,2048]{1,0:T(8,128)(2,1)S(1)}, u32[]{:S(2)}, u32[]{:S(2)}) %collective-permute-start.4) | collective-permute-done | bytes 131104 | tf_op jit(solution)/shard_map/ppermute | solution.py:289
  24.6 4.0 collective-permute-start.9
  28.7 11.1 %collective-permute-done.8.refs_1_ = bf16[2,2,32,2048]{3,2,1,0:T(8,128)(2,1)} collective-permute-done((bf16[2,2,32,2048]{3,2,1,0:T(8,128)(2,1)S(1)}, bf16[2,2,32,2048]{3,2,1,0:T(8,128)(2,1)}, u32[]{:S(2)}, u32[]{:S(2)}) %collective-permute-start.8) | collective-permute-done | bytes 524320 | tf_op jit(solution)/shard_map/ppermute | solution.py:293
  43.5 3.5 collective-permute-done.32
  46.9 27.6 %all-gather.3.cloned.1.call-done = bf16[256,2048]{1,0:T(8,128)(2,1)} async-done(((bf16[32,2048]{1,0:T(8,128)(2,1)}), bf16[256,2048]{1,0:T(8,128)(2,1)}) %all-gather.3.cloned.1.call-update) | async-done | bytes 1048592 | tf_op jit(solution)/shard_map/all_gather | solution.py:321
  81.1 5.7 %collective-permute-done.12.refs_5_ = bf16[2,2,32,2048]{3,2,1,0:T(8,128)(2,1)S(1)} collective-permute-done((bf16[2,2,32,2048]{3,2,1,0:T(8,128)(2,1)}, bf16[2,2,32,2048]{3,2,1,0:T(8,128)(2,1)S(1)}, u32[]{:S(2)}, u32[]{:S(2)}) %collective-permute-start.12) | collective-permute-done | bytes 524320 | tf_op jit(solution)/shard_map/ppermute | solution.py:293
  91.6 6.4 %collective-permute-done.1.refs_11_ = bf16[8,32,2048]{2,1,0:T(8,128)(2,1)S(1)} collective-permute-done((bf16[8,32,2048]{2,1,0:T(8,128)(2,1)}, bf16[8,32,2048]{2,1,0:T(8,128)(2,1)S(1)}, u32[]{:S(2)}, u32[]{:S(2)}) %collective-permute-start.1) | collective-permute-done | bytes 1048608 | tf_op jit(solution)/shard_map/ppermute | solution.py:289
  100.1 4.2 collective-permute-done.15.refs_8_
  106.8 8.8 %collective-permute-done.2.refs_13_ = bf16[4,32,2048]{2,1,0:T(8,128)(2,1)S(1)} collective-permute-done((bf16[4,32,2048]{2,1,0:T(8,128)(2,1)S(1)}, bf16[4,32,2048]{2,1,0:T(8,128)(2,1)S(1)}, u32[]{:S(2)}, u32[]{:S(2)}) %collective-permute-start.2) | collective-permute-done | bytes 524320 | tf_op jit(solution)/shard_map/ppermute | solution.py:289
  124.8 5.4 %select_reduce_fusion.4 = (f32[64,2048]{1,0:T(8,128)}, f32[64,2048]{1,0:T(8,128)}, f32[64,2048]{1,0:T(8,128)}, f32[64,2048]{1,0:T(8,128)}, f32[64,2048]{1,0:T(8,...) fusion(f32[2,64,2048]{2,1,0:T(8,128)} %param.8, ...), kind=kLoop, calls=%fused_computation.29 | loop fusion | flops 3538944 | bytes 7864326 | tf_op jit(solution)/shard_map/reduce_sum | solution.py:414
  134.4 9.9 %forward_tick.5 = (bf16[64,2048]{1,0:T(8,128)(2,1)}, bf16[2,128,2048]{2,1,0:T(8,128)(2,1)}, f32[2,128,2048]{2,1,0:T(8,128)}) custom-call(s32[8]{0:T(128)} %stack.299.ctl, bf16[2,2,32,2048]{3,2,1,0:T(8,128)(2,1)} %copy-done.3, bf16[2,2,32,2048]{3,2,1,0:T(8,128)(2,1)} %collective-permute-done.8.refs_1_, ...), custom_call_target="tpu_custom_call", output_to_operand_aliasing={{1}: (32, {}), {2}: (33, {})} | custom-call | flops 1073741824 | bytes 16777216 | tf_op jit(solution)/shard_map/forward_tick/pallas_call | solution.py:219
  145.9 9.8 %collective-permute-start.3 = (f32[3,64,2048]{2,1,0:T(8,128)S(1)}, f32[3,64,2048]{2,1,0:T(8,128)}, u32[]{:S(2)}, u32[]{:S(2)}) collective-permute-start(f32[3,64,2048]{2,1,0:T(8,128)S(1)} %pad_maximum_fusion), channel_id=1, source_target_pairs={{0,32},{32,0},{1,33},{33,1},{2,34},{34,2},{3,35},{35,3},{4,36},{36... | collective-permute-start | bytes 4718600 | tf_op jit(solution)/shard_map/ppermute | solution.py:301
  156.4 9.9 %forward_tick.6 = (bf16[64,2048]{1,0:T(8,128)(2,1)}, bf16[2,128,2048]{2,1,0:T(8,128)(2,1)}, f32[2,128,2048]{2,1,0:T(8,128)}) custom-call(s32[8]{0:T(128)} %stack.295.ctl, bf16[2,2,32,2048]{3,2,1,0:T(8,128)(2,1)} %copy-done.3, bf16[2,2,32,2048]{3,2,1,0:T(8,128)(2,1)} %collective-permute-done.8.refs_1_, ...), custom_call_target="tpu_custom_call", output_to_operand_aliasing={{1}: (32, {}), {2}: (33, {})} | custom-call | flops 1073741824 | bytes 16777216 | tf_op jit(solution)/shard_map/forward_tick/pallas_call | solution.py:219
  203.4 66.4 %collective-permute-done.43.refs_29_ = bf16[64,2048]{1,0:T(8,128)(2,1)S(1)} collective-permute-done((bf16[64,2048]{1,0:T(8,128)(2,1)}, bf16[64,2048]{1,0:T(8,128)(2,1)S(1)}, u32[]{:S(2)}, u32[]{:S(2)}) %collective-permute-start.43) | collective-permute-done | bytes 262176 | tf_op jit(solution)/shard_map/ppermute | solution.py:475
  270.6 9.2 %backward_tick.8 = (bf16[64,2048]{1,0:T(8,128)(2,1)}, bf16[2,128,2048]{2,1,0:T(8,128)(2,1)}) custom-call(s32[8]{0:T(128)} %stack.307.ctl, bf16[2,2,32,2048]{3,2,1,0:T(8,128)(2,1)} %copy-done.3, bf16[2,2,32,2048]{3,2,1,0:T(8,128)(2,1)} %collective-permute-done.8.refs_1_, ...), custom_call_target="tpu_custom_call", output_to_operand_aliasing={{1}: (34, {})} | custom-call | flops 1073741824 | bytes 16777216 | tf_op jit(solution)/shard_map/backward_tick/pallas_call | solution.py:250
  280.9 23.7 %collective-permute-start.47 = (bf16[64,2048]{1,0:T(8,128)(2,1)S(1)}, bf16[64,2048]{1,0:T(8,128)(2,1)S(1)}, u32[]{:S(2)}, u32[]{:S(2)}) collective-permute-start(bf16[64,2048]{1,0:T(8,128)(2,1)S(1)} %get-tuple-element.89), channel_id=1, source_target_pairs={{0,32},{32,2},{2,34},{34,0},{1,33},{33,3},{3,35},{35,1},{4,36},{36... | collective-permute-start | bytes 786440 | tf_op jit(solution)/shard_map/ppermute | solution.py:289
  311.4 17.6 %collective-permute-done.44.refs_29_ = bf16[64,2048]{1,0:T(8,128)(2,1)S(1)} collective-permute-done((bf16[64,2048]{1,0:T(8,128)(2,1)S(1)}, bf16[64,2048]{1,0:T(8,128)(2,1)S(1)}, u32[]{:S(2)}, u32[]{:S(2)}) %collective-permute-start.44) | collective-permute-done | bytes 262176 | tf_op jit(solution)/shard_map/ppermute | solution.py:475
  329.7 9.2 %backward_tick.9 = (bf16[64,2048]{1,0:T(8,128)(2,1)}, bf16[2,128,2048]{2,1,0:T(8,128)(2,1)}) custom-call(s32[8]{0:T(128)} %stack.323.ctl, bf16[2,2,32,2048]{3,2,1,0:T(8,128)(2,1)} %copy-done.3, bf16[2,2,32,2048]{3,2,1,0:T(8,128)(2,1)} %collective-permute-done.8.refs_1_, ...), custom_call_target="tpu_custom_call", output_to_operand_aliasing={{1}: (34, {})} | custom-call | flops 1073741824 | bytes 16777216 | tf_op jit(solution)/shard_map/backward_tick/pallas_call | solution.py:250
  344.9 9.8 %collective-permute-done.48.refs_5_ = bf16[64,2048]{1,0:T(8,128)(2,1)S(1)} collective-permute-done((bf16[64,2048]{1,0:T(8,128)(2,1)S(1)}, bf16[64,2048]{1,0:T(8,128)(2,1)S(1)}, u32[]{:S(2)}, u32[]{:S(2)}) %collective-permute-start.48) | collective-permute-done | bytes 262176 | tf_op jit(solution)/shard_map/ppermute | solution.py:289
  361.4 8.4 %weight_grads.1 = bf16[8,64,2048]{2,1,0:T(8,128)(2,1)} custom-call(bf16[512,1024]{1,0:T(8,128)(2,1)} %bitcast.165, bf16[64,2048]{1,0:T(8,128)(2,1)} %copy-done.36, bf16[64,2048]{1,0:T(8,128)(2,1)} %copy-done.37, bf16[64,2048]{1,0:T(8,128)(2,1)} %copy-done.41, bf16[64,2048]{1,0:T(8,128)(2,1)} %copy-done.43, bf16[64,2048]{1,0:T(8,128)(2,1)} %copy-done.39, ...), custom_call_target="tpu_custom_call" | custom-call | flops 2147483648 | bytes 7340032 | tf_op jit(solution)/shard_map/weight_grads/pallas_call | solution.py:367
  382.4 5.4 %collective-permute-done.60 = bf16[64,2048]{1,0:T(8,128)(2,1)S(1)} collective-permute-done((bf16[64,2048]{1,0:T(8,128)(2,1)S(1)}, bf16[64,2048]{1,0:T(8,128)(2,1)S(1)}, u32[]{:S(2)}, u32[]{:S(2)}) %collective-permute-start.60) | collective-permute-done | bytes 262176 | tf_op jit(solution)/shard_map/ppermute | solution.py:293
  388.0 7.8 %collective-permute-done.61 = bf16[64,2048]{1,0:T(8,128)(2,1)S(1)} collective-permute-done((bf16[64,2048]{1,0:T(8,128)(2,1)S(1)}, bf16[64,2048]{1,0:T(8,128)(2,1)S(1)}, u32[]{:S(2)}, u32[]{:S(2)}) %collective-permute-start.61) | collective-permute-done | bytes 262176 | tf_op jit(solution)/shard_map/ppermute | solution.py:293
  398.6 4.4 %collective-permute-done.65 = bf16[64,2048]{1,0:T(8,128)(2,1)S(1)} collective-permute-done((bf16[64,2048]{1,0:T(8,128)(2,1)S(1)}, bf16[64,2048]{1,0:T(8,128)(2,1)S(1)}, u32[]{:S(2)}, u32[]{:S(2)}) %collective-permute-start.65) | collective-permute-done | bytes 262176 | tf_op jit(solution)/shard_map/ppermute | solution.py:293
  406.5 4.0 collective-permute-done.66
  (291 shorter events, 125.1 us)
Async XLA Ops:
  7.2 67.4 %all-gather.3.cloned.1.call-start = ((), (), s32[]{:S(2)}) async-start(), calls=%async_computation | async-start | bytes 1179648 | tf_op jit(solution)/shard_map/all_gather | solution.py:321
  22.6 17.1 %collective-permute-start.8 = (bf16[2,2,32,2048]{3,2,1,0:T(8,128)(2,1)S(1)}, bf16[2,2,32,2048]{3,2,1,0:T(8,128)(2,1)}, u32[]{:S(2)}, u32[]{:S(2)}) collective-permute-start(bf16[2,2,32,2048]{3,2,1,0:T(8,128)(2,1)S(1)} %pad_maximum_fusion.2.refs_0_), channel_id=1, source_target_pairs={{0,4},{4,8},{8,12},{12,16},{16,20},{20,24},{24,28},{28,0},{1,5},{5... | collective-permute-start | bytes 1572872 | tf_op jit(solution)/shard_map/ppermute | solution.py:293
  39.8 35.1 %collective-permute-start.10 = (bf16[2,2,32,2048]{3,2,1,0:T(8,128)(2,1)}, bf16[2,2,32,2048]{3,2,1,0:T(8,128)(2,1)}, u32[]{:S(2)}, u32[]{:S(2)}) collective-permute-start(bf16[2,2,32,2048]{3,2,1,0:T(8,128)(2,1)} %collective-permute-done.8.refs_1_), channel_id=1, source_target_pairs={{0,4},{4,8},{8,12},{12,16},{16,20},{20,24},{24,28},{28,0},{1,5},{5... | collective-permute-start | bytes 1572872 | tf_op jit(solution)/shard_map/ppermute | solution.py:293
  39.8 36.7 %collective-permute-start.18 = (bf16[2,2,32,2048]{3,2,1,0:T(8,128)(2,1)S(1)}, bf16[2,2,32,2048]{3,2,1,0:T(8,128)(2,1)}, u32[]{:S(2)}, u32[]{:S(2)}) collective-permute-start(bf16[2,2,32,2048]{3,2,1,0:T(8,128)(2,1)S(1)} %pad_maximum_fusion.2.refs_0_), channel_id=1, source_target_pairs={{0,1},{1,0},{2,3},{3,2},{4,5},{5,4},{6,7},{7,6},{8,9},{9,8},{10,11... | collective-permute-start | bytes 1572872 | tf_op jit(solution)/shard_map/ppermute | solution.py:297
  39.8 39.3 %collective-permute-start.11 = (bf16[2,2,32,2048]{3,2,1,0:T(8,128)(2,1)}, bf16[2,2,32,2048]{3,2,1,0:T(8,128)(2,1)}, u32[]{:S(2)}, u32[]{:S(2)}) collective-permute-start(bf16[2,2,32,2048]{3,2,1,0:T(8,128)(2,1)} %collective-permute-done.9.refs_2_), channel_id=1, source_target_pairs={{0,28},{4,0},{8,4},{12,8},{16,12},{20,16},{24,20},{28,24},{1,29},{... | collective-permute-start | bytes 1572872 | tf_op jit(solution)/shard_map/ppermute | solution.py:293
  43.2 37.9 %collective-permute-start.19 = (bf16[2,2,32,2048]{3,2,1,0:T(8,128)(2,1)}, bf16[2,2,32,2048]{3,2,1,0:T(8,128)(2,1)}, u32[]{:S(2)}, u32[]{:S(2)}) collective-permute-start(bf16[2,2,32,2048]{3,2,1,0:T(8,128)(2,1)} %collective-permute-done.8.refs_1_), channel_id=1, source_target_pairs={{0,1},{1,0},{2,3},{3,2},{4,5},{5,4},{6,7},{7,6},{8,9},{9,8},{10,11... | collective-permute-start | bytes 1572872 | tf_op jit(solution)/shard_map/ppermute | solution.py:297
  74.6 23.4 %collective-permute-start.1 = (bf16[8,32,2048]{2,1,0:T(8,128)(2,1)}, bf16[8,32,2048]{2,1,0:T(8,128)(2,1)S(1)}, u32[]{:S(2)}, u32[]{:S(2)}) collective-permute-start(bf16[8,32,2048]{2,1,0:T(8,128)(2,1)} %bitcast.151), channel_id=1, source_target_pairs={{0,34},{32,0},{2,32},{34,2},{1,35},{33,1},{3,33},{35,3},{4,38},{36... | collective-permute-start | bytes 3145736 | tf_op jit(solution)/shard_map/ppermute | solution.py:289
  76.5 27.9 %collective-permute-start.16 = (bf16[8,32,2048]{2,1,0:T(8,128)(2,1)}, bf16[8,32,2048]{2,1,0:T(8,128)(2,1)S(1)}, u32[]{:S(2)}, u32[]{:S(2)}) collective-permute-start(bf16[8,32,2048]{2,1,0:T(8,128)(2,1)} %bitcast.152), channel_id=1, source_target_pairs={{0,32},{32,2},{2,34},{34,0},{1,33},{33,3},{3,35},{35,1},{4,36},{36... | collective-permute-start | bytes 3145736 | tf_op jit(solution)/shard_map/ppermute | solution.py:289
  100.1 15.5 %collective-permute-start.2 = (bf16[4,32,2048]{2,1,0:T(8,128)(2,1)S(1)}, bf16[4,32,2048]{2,1,0:T(8,128)(2,1)S(1)}, u32[]{:S(2)}, u32[]{:S(2)}) collective-permute-start(bf16[4,32,2048]{2,1,0:T(8,128)(2,1)S(1)} %slice.133), channel_id=1, source_target_pairs={{0,34},{32,0},{2,32},{34,2},{1,35},{33,1},{3,33},{35,3},{4,38},{36... | collective-permute-start | bytes 1572872 | tf_op jit(solution)/shard_map/ppermute | solution.py:289
  105.7 18.4 %collective-permute-start.24 = (bf16[2,2,32,2048]{3,2,1,0:T(8,128)(2,1)}, bf16[2,2,32,2048]{3,2,1,0:T(8,128)(2,1)}, u32[]{:S(2)}, u32[]{:S(2)}) collective-permute-start(bf16[2,2,32,2048]{3,2,1,0:T(8,128)(2,1)} %collective-permute-done.13.refs_6_), channel_id=1, source_target_pairs={{0,1},{1,0},{2,3},{3,2},{4,5},{5,4},{6,7},{7,6},{8,9},{9,8},{10,11... | collective-permute-start | bytes 1572872 | tf_op jit(solution)/shard_map/ppermute | solution.py:297
  105.9 18.8 %collective-permute-start.17 = (bf16[4,32,2048]{2,1,0:T(8,128)(2,1)}, bf16[4,32,2048]{2,1,0:T(8,128)(2,1)}, u32[]{:S(2)}, u32[]{:S(2)}) collective-permute-start(bf16[4,32,2048]{2,1,0:T(8,128)(2,1)} %slice.141), channel_id=1, source_target_pairs={{0,32},{32,2},{2,34},{34,0},{1,33},{33,3},{3,35},{35,1},{4,36},{36... | collective-permute-start | bytes 1572872 | tf_op jit(solution)/shard_map/ppermute | solution.py:289
  106.2 23.9 %collective-permute-start.27 = (bf16[8,32,2048]{2,1,0:T(8,128)(2,1)S(1)}, bf16[8,32,2048]{2,1,0:T(8,128)(2,1)}, u32[]{:S(2)}, u32[]{:S(2)}) collective-permute-start(bf16[8,32,2048]{2,1,0:T(8,128)(2,1)S(1)} %bitcast.163), channel_id=1, source_target_pairs={{0,1},{1,0},{2,3},{3,2},{4,5},{5,4},{6,7},{7,6},{8,9},{9,8},{10,11... | collective-permute-start | bytes 3145736 | tf_op jit(solution)/shard_map/ppermute | solution.py:297
  106.4 23.8 %collective-permute-start.28 = (bf16[8,32,2048]{2,1,0:T(8,128)(2,1)S(1)}, bf16[8,32,2048]{2,1,0:T(8,128)(2,1)}, u32[]{:S(2)}, u32[]{:S(2)}) collective-permute-start(bf16[8,32,2048]{2,1,0:T(8,128)(2,1)S(1)} %collective-permute-done.16.refs_10_), channel_id=1, source_target_pairs={{0,1},{1,0},{2,3},{3,2},{4,5},{5,4},{6,7},{7,6},{8,9},{9,8},{10,11... | collective-permute-start | bytes 3145736 | tf_op jit(solution)/shard_map/ppermute | solution.py:297
  145.9 50.2 %collective-permute-start.3 = (f32[3,64,2048]{2,1,0:T(8,128)S(1)}, f32[3,64,2048]{2,1,0:T(8,128)}, u32[]{:S(2)}, u32[]{:S(2)}) collective-permute-start(f32[3,64,2048]{2,1,0:T(8,128)S(1)} %pad_maximum_fusion), channel_id=1, source_target_pairs={{0,32},{32,0},{1,33},{33,1},{2,34},{34,2},{3,35},{35,3},{4,36},{36... | collective-permute-start | bytes 4718600 | tf_op jit(solution)/shard_map/ppermute | solution.py:301
  168.9 27.3 %collective-permute-start.5 = (f32[3,64,2048]{2,1,0:T(8,128)}, f32[3,64,2048]{2,1,0:T(8,128)}, u32[]{:S(2)}, u32[]{:S(2)}) collective-permute-start(f32[3,64,2048]{2,1,0:T(8,128)} %pad_maximum_fusion.1), channel_id=1, source_target_pairs={{96,128},{128,96},{97,129},{129,97},{98,130},{130,98},{99,131},{13... | collective-permute-start | bytes 4718600 | tf_op jit(solution)/shard_map/ppermute | solution.py:305
  193.3 76.5 %collective-permute-start.43 = (bf16[64,2048]{1,0:T(8,128)(2,1)}, bf16[64,2048]{1,0:T(8,128)(2,1)S(1)}, u32[]{:S(2)}, u32[]{:S(2)}) collective-permute-start(bf16[64,2048]{1,0:T(8,128)(2,1)} %get-tuple-element.44), channel_id=1, source_target_pairs={{64,0},{128,64},{65,1},{129,65},{66,2},{130,66},{67,3},{131,67},{6... | collective-permute-start | bytes 786440 | tf_op jit(solution)/shard_map/ppermute | solution.py:475
  199.5 105.9 %collective-permute-start.38 = (bf16[8,64,256]{2,1,0:T(8,128)(2,1)S(1)}, bf16[8,64,256]{2,1,0:T(8,128)(2,1)S(1)}, u32[]{:S(2)}, u32[]{:S(2)}) collective-permute-start(bf16[8,64,256]{2,1,0:T(8,128)(2,1)S(1)} %get-tuple-element.83), channel_id=1, source_target_pairs={{0,32},{32,2},{2,34},{34,0},{1,33},{33,3},{3,35},{35,1},{4,36},{36... | collective-permute-start | bytes 786440 | tf_op jit(solution)/shard_map/ppermute | solution.py:289
  199.6 105.8 %collective-permute-start.39 = (bf16[8,64,256]{2,1,0:T(8,128)(2,1)S(1)}, bf16[8,64,256]{2,1,0:T(8,128)(2,1)S(1)}, u32[]{:S(2)}, u32[]{:S(2)}) collective-permute-start(bf16[8,64,256]{2,1,0:T(8,128)(2,1)S(1)} %get-tuple-element.84), channel_id=1, source_target_pairs={{0,34},{32,0},{2,32},{34,2},{1,35},{33,1},{3,33},{35,3},{4,38},{36... | collective-permute-start | bytes 786440 | tf_op jit(solution)/shard_map/ppermute | solution.py:289
  201.6 105.9 %collective-permute-start.40 = (bf16[8,64,256]{2,1,0:T(8,128)(2,1)S(1)}, bf16[8,64,256]{2,1,0:T(8,128)(2,1)S(1)}, u32[]{:S(2)}, u32[]{:S(2)}) collective-permute-start(bf16[8,64,256]{2,1,0:T(8,128)(2,1)S(1)} %get-tuple-element.81), channel_id=1, source_target_pairs={{0,2},{32,34},{2,0},{34,32},{1,3},{33,35},{3,1},{35,33},{4,6},{36,... | collective-permute-start | bytes 786440 | tf_op jit(solution)/shard_map/ppermute | solution.py:289
  280.9 61.9 %collective-permute-start.47 = (bf16[64,2048]{1,0:T(8,128)(2,1)S(1)}, bf16[64,2048]{1,0:T(8,128)(2,1)S(1)}, u32[]{:S(2)}, u32[]{:S(2)}) collective-permute-start(bf16[64,2048]{1,0:T(8,128)(2,1)S(1)} %get-tuple-element.89), channel_id=1, source_target_pairs={{0,32},{32,2},{2,34},{34,0},{1,33},{33,3},{3,35},{35,1},{4,36},{36... | collective-permute-start | bytes 786440 | tf_op jit(solution)/shard_map/ppermute | solution.py:289
  304.6 38.4 %collective-permute-start.51 = (bf16[64,2048]{1,0:T(8,128)(2,1)S(1)}, bf16[64,2048]{1,0:T(8,128)(2,1)S(1)}, u32[]{:S(2)}, u32[]{:S(2)}) collective-permute-start(bf16[64,2048]{1,0:T(8,128)(2,1)S(1)} %get-tuple-element.89), channel_id=1, source_target_pairs={{0,34},{32,0},{2,32},{34,2},{1,35},{33,1},{3,33},{35,3},{4,38},{36... | collective-permute-start | bytes 786440 | tf_op jit(solution)/shard_map/ppermute | solution.py:289
  305.5 34.7 %collective-permute-start.45 = (bf16[64,2048]{1,0:T(8,128)(2,1)S(1)}, bf16[64,2048]{1,0:T(8,128)(2,1)S(1)}, u32[]{:S(2)}, u32[]{:S(2)}) collective-permute-start(bf16[64,2048]{1,0:T(8,128)(2,1)S(1)} %get-tuple-element.90.refs_0_), channel_id=1, source_target_pairs={{0,1},{1,0},{2,3},{3,2},{4,5},{5,4},{6,7},{7,6},{8,9},{9,8},{10,11... | collective-permute-start | bytes 786440 | tf_op jit(solution)/shard_map/ppermute | solution.py:297
  305.5 37.6 %collective-permute-start.55 = (bf16[64,2048]{1,0:T(8,128)(2,1)S(1)}, bf16[64,2048]{1,0:T(8,128)(2,1)S(1)}, u32[]{:S(2)}, u32[]{:S(2)}) collective-permute-start(bf16[64,2048]{1,0:T(8,128)(2,1)S(1)} %get-tuple-element.90.refs_0_), channel_id=1, source_target_pairs={{0,2},{32,34},{2,0},{34,32},{1,3},{33,35},{3,1},{35,33},{4,6},{36,... | collective-permute-start | bytes 786440 | tf_op jit(solution)/shard_map/ppermute | solution.py:289
  307.6 21.5 %collective-permute-start.44 = (bf16[64,2048]{1,0:T(8,128)(2,1)S(1)}, bf16[64,2048]{1,0:T(8,128)(2,1)S(1)}, u32[]{:S(2)}, u32[]{:S(2)}) collective-permute-start(bf16[64,2048]{1,0:T(8,128)(2,1)S(1)} %copy-done.50), channel_id=1, source_target_pairs={{64,0},{65,1},{66,2},{67,3},{68,4},{69,5},{70,6},{71,7},{72,8},{73... | collective-permute-start | bytes 786440 | tf_op jit(solution)/shard_map/ppermute | solution.py:475
  (99 other events, 1203.3 us)
Sparse Core Ops, SparseCore 0:
  21.2 53.3 all-gather.2
